TPU v7x, 256 devices: a whole 4x4x8 slice. The times are simulated.
256 devices in a mesh: row: 16 (over x, y), col: 16 (over z, core).
Axes of the slice: x: 4, y: 4, z: 8, core: 2. Of those that a mesh axis runs over, the one named last changes fastest.
Arguments:
- inducing_desc: bfloat16 [2, 1960, 2048], P(None, None, 'row'), may hold values from -0.8984375 to 0.8984375
- candidate_desc: bfloat16 [1960, 12288], P(None, 'col'), may hold values from -0.8984375 to 0.8984375
- first_inverse: float32 [2048, 2048], P('row', 'col'), may hold values from -2 to 2, as said below
- coupling: float32 [2048, 2048], P('row', 'col'), may hold values from -0.0625 to 0.0625
- second_inverse: float32 [2048, 2048], P('row', 'col'), may hold values from -2 to 2, as said below
Outputs:
- first_solved: float32 [2048, 12288], P('row', 'col')
- second_solved: float32 [2048, 12288], P('row', 'col')
- explained: float32 [12288], P('col')
Inputs may be any that keep to these rules, and one draw needn't show every extreme that they name: `first_inverse`: lower triangular: zero above the diagonal, positive on it. `second_inverse`: lower triangular: zero above the diagonal, positive on it.
All inputs are finite; a program needn't handle non-finite values.
Results may differ from a plain program's by a relative error of at most 0.0003.
Values may be sent and summed in bfloat16 or wider, within the bound.
A program may use at most 128 MiB of HBM per device.

v0:
```python
import jax
import jax.numpy as jnp
from jax import lax
from jax.sharding import PartitionSpec as P

B = 2048


def product(left, right):
    return jnp.dot(left, right, precision=lax.Precision.HIGHEST, preferred_element_type=jnp.float32)


def fold_with(block_rows, piece):
    return product(block_rows, piece)


def shards(inducing_desc, candidate_desc, first_inverse, coupling, second_inverse):
    share = inducing_desc.shape[2]
    inverse_one = lax.all_gather(first_inverse, "col", axis=1, tiled=True)
    inverse_two = lax.all_gather(second_inverse, "col", axis=1, tiled=True)
    link_rows = lax.all_gather(coupling, "col", axis=1, tiled=True)
    inner = jnp.einsum(
        "pwn,wc->pnc",
        lax.all_gather(inducing_desc, "row", axis=2, tiled=True),
        candidate_desc,
        preferred_element_type=jnp.float32,
    )
    kernels = inner * inner
    first_solved = product(inverse_one, kernels[0])
    begin = lax.axis_index("row") * share
    second_kernel = lax.dynamic_slice_in_dim(kernels[1], begin, share, 0)
    remainder = second_kernel - fold_with(
        link_rows, lax.all_gather(first_solved, "row", axis=0, tiled=True)
    )
    second_solved = fold_with(inverse_two, lax.all_gather(remainder, "row", axis=0, tiled=True))
    partial_sums = jnp.sum(first_solved * first_solved, axis=0) + jnp.sum(
        second_solved * second_solved, axis=0
    )
    explained = lax.psum(partial_sums, "row") / (2.0 * B)
    return (first_solved, second_solved, explained)


def solution(mesh):
    return jax.shard_map(
        shards,
        mesh=mesh,
        in_specs=(
            P(None, None, "row"),
            P(None, "col"),
            P("row", "col"),
            P("row", "col"),
            P("row", "col"),
        ),
        out_specs=(P("row", "col"), P("row", "col"), P("col")),
        check_vma=False,
    )
```

profile of v0, /device:TPU:32, one launch (start us, length us, event | category | flops | bytes accessed | tf_op | source)
XLA Modules:
  0.0 441.9 jit_solution(2902040982423365451)
XLA Ops:
  7.2 0.0 all-gather.7.cloned.1.call-start
  7.2 0.7 all-gather.7.cloned.1.call-update
  7.9 0.0 all-gather.9.cloned.1.call-start
  8.0 0.7 all-gather.9.cloned.1.call-update
  8.7 0.0 all-gather.13.cloned.1.call-start
  8.7 0.7 all-gather.13.cloned.1.call-update
  9.4 0.0 all-gather.11.cloned.1.call-start
  9.4 126.0 %all-gather.7.cloned.1.call-done = bf16[2,1960,2048]{2,1,0:T(8,128)(2,1)} async-done(((bf16[2,1960,128]{2,1,0:T(8,128)(2,1)}), bf16[2,1960,2048]{2,1,0:T(8,128)(2,1)}) %all-gather.7.cloned.1.call-update) | async-done | bytes 16056336 | tf_op jit(solution)/shard_map/all_gather | solution.py:24
  135.4 18.5 %convolution_multiply_fusion = f32[2,2048,768]{2,1,0:T(8,128)} fusion(bf16[2,1960,2048]{2,1,0:T(8,128)(2,1)} %all-gather.7.cloned.1.call-done, bf16[1960,768]{1,0:T(8,128)(2,1)S(1)} %copy-done), kind=kOutput, calls=%fused_computation | convolution fusion | flops 12334399488 | bytes 31649792 | tf_op jit(solution)/shard_map/pwn,wc->pnc/dot_general | solution.py:22
  153.9 19.9 %all-gather.9.cloned.1.call-done = f32[128,2048]{1,0:T(8,128)} async-done(((f32[128,128]{1,0:T(8,128)}), f32[128,2048]{1,0:T(8,128)}) %all-gather.9.cloned.1.call-update) | async-done | bytes 1048592 | tf_op jit(solution)/shard_map/all_gather | solution.py:19
  173.9 7.5 %multiply_reduce_fusion.1 = (f32[768]{0:T(1024)S(1)}, f32[128,768]{1,0:T(8,128)}) fusion(f32[128,2048]{1,0:T(8,128)} %all-gather.9.cloned.1.call-done, f32[2,2048,768]{2,1,0:T(8,128)} %convolution_multiply_fusion), kind=kOutput, calls=%fused_computation.9 | convolution fusion | flops 2416114944 | bytes 7736320 | tf_op jit(solution)/shard_map/dot_general | solution.py:10
  181.3 0.0 all-gather.11.cloned.1.call-update
  181.4 0.0 all-gather.17.cloned.1.call-start
  181.4 0.5 all-gather.17.cloned.1.call-update
  182.0 0.2 all-gather.15.cloned.1.call-start
  182.2 5.8 %slice.9 = f32[1,2048,768]{2,1,0:T(8,128)} slice(f32[2,2048,768]{2,1,0:T(8,128)} %convolution_multiply_fusion), slice={[1:2], [0:2048], [0:768]} | slice | bytes 12582912 | tf_op jit(solution)/shard_map/slice | solution.py:31
  188.0 24.4 %all-gather.13.cloned.1.call-done = f32[128,2048]{1,0:T(8,128)} async-done(((f32[128,128]{1,0:T(8,128)}), f32[128,2048]{1,0:T(8,128)}) %all-gather.13.cloned.1.call-update) | async-done | bytes 1048592 | tf_op jit(solution)/shard_map/all_gather | solution.py:21
  212.4 68.8 %all-gather.11.cloned.1.call-done = f32[2048,768]{1,0:T(8,128)} async-done(((f32[128,768]{1,0:T(8,128)}), f32[2048,768]{1,0:T(8,128)}) %all-gather.11.cloned.1.call-update) | async-done | bytes 6291472 | tf_op jit(solution)/shard_map/all_gather | solution.py:33
  281.2 7.5 %fusion.3 = f32[128,768]{1,0:T(8,128)} fusion(f32[2048,768]{1,0:T(8,128)} %all-gather.11.cloned.1.call-done, f32[128,2048]{1,0:T(8,128)} %all-gather.13.cloned.1.call-done, f32[1,2048,768]{2,1,0:T(8,128)} %slice.9, s32[]{:T(128)S(6)} %select_n.3), kind=kOutput, calls=%fused_computation.7 | convolution fusion | flops 2416017408 | bytes 8126468 | tf_op jit(solution)/shard_map/dot_general | solution.py:10
  288.8 31.0 %all-gather.17.cloned.1.call-done = f32[128,2048]{1,0:T(8,128)} async-done(((f32[128,128]{1,0:T(8,128)}), f32[128,2048]{1,0:T(8,128)}) %all-gather.17.cloned.1.call-update) | async-done | bytes 1048592 | tf_op jit(solution)/shard_map/all_gather | solution.py:20
  319.8 68.8 %all-gather.15.cloned.1.call-done = f32[2048,768]{1,0:T(8,128)} async-done(((f32[128,768]{1,0:T(8,128)}), f32[2048,768]{1,0:T(8,128)}) %all-gather.15.cloned.1.call-update) | async-done | bytes 6291472 | tf_op jit(solution)/shard_map/all_gather | solution.py:35
  388.6 7.5 %multiply_reduce_fusion = (f32[768]{0:T(1024)S(1)}, f32[128,768]{1,0:T(8,128)}) fusion(f32[2048,768]{1,0:T(8,128)} %all-gather.15.cloned.1.call-done, f32[128,2048]{1,0:T(8,128)} %all-gather.17.cloned.1.call-done), kind=kOutput, calls=%fused_computation.8 | convolution fusion | flops 2416114944 | bytes 7736320 | tf_op jit(solution)/shard_map/dot_general | solution.py:10
  396.1 38.4 %psum.7 = f32[768]{0:T(1024)S(1)} all-reduce(f32[768]{0:T(1024)S(1)} %add.9), channel_id=1, replica_groups=mesh['row'=16,'col'=16] {'row'}, use_global_device_ids=true, to_apply=%region_2.0 | all-reduce | flops 768 | bytes 6144 | tf_op jit(solution)/shard_map/psum | solution.py:39
  434.5 0.6 broadcast_multiply_fusion
  (4 shorter events, 0.0 us)
Async XLA Ops:
  7.2 128.3 %copy-start = (bf16[1960,768]{1,0:T(8,128)(2,1)S(1)}, bf16[1960,768]{1,0:T(8,128)(2,1)}, u32[]{:S(2)}) copy-start(bf16[1960,768]{1,0:T(8,128)(2,1)} %param.6) | copy-start | bytes 9031684
  7.2 128.2 %all-gather.7.cloned.1.call-start = ((), (), s32[]{:S(2)}) async-start(), calls=%async_computation | async-start | bytes 17059840 | tf_op jit(solution)/shard_map/all_gather | solution.py:24
  7.9 166.0 %all-gather.9.cloned.1.call-start = ((), (), s32[]{:S(2)}) async-start(), calls=%async_computation.1 | async-start | bytes 1114112 | tf_op jit(solution)/shard_map/all_gather | solution.py:19
  8.7 203.7 %all-gather.13.cloned.1.call-start = ((), (), s32[]{:S(2)}) async-start(), calls=%async_computation.3 | async-start | bytes 1114112 | tf_op jit(solution)/shard_map/all_gather | solution.py:21
  9.4 271.8 %all-gather.11.cloned.1.call-start = ((), (), s32[]{:S(2)}) async-start(), calls=%async_computation.2 | async-start | bytes 6684672 | tf_op jit(solution)/shard_map/all_gather | solution.py:33
  181.4 138.4 %all-gather.17.cloned.1.call-start = ((), (), s32[]{:S(2)}) async-start(), calls=%async_computation.5 | async-start | bytes 1114112 | tf_op jit(solution)/shard_map/all_gather | solution.py:20
  182.0 206.7 %all-gather.15.cloned.1.call-start = ((), (), s32[]{:S(2)}) async-start(), calls=%async_computation.4 | async-start | bytes 6684672 | tf_op jit(solution)/shard_map/all_gather | solution.py:35
Sparse Core Ops, SparseCore 0:
  10.4 124.9 all-gather.6
  137.2 36.6 all-gather.8
  175.6 36.7 all-gather.12
  215.3 65.8 all-gather.10
  282.8 36.9 all-gather.16
  322.7 65.8 all-gather.14
where the time goes:
time: 442 us
  waiting for transfers between devices  342 us (77%)
  matrix products  41 us (9%)
  blocking collectives  38.4 us (9%)
  between operations  14.1 us (3%)
  local copies, waits for them, and re-layouts  5.84 us (1%)
    all_gather x1, waiting for transfers between devices, shards(): lax.all_gather(inducing_desc, 'row', axis=2, tiled=True)  126 us
    all_gather x1, waiting for transfers between devices, shards(): lax.all_gather(remainder, 'row', axis=0, tiled=True)  68.8 us
    all_gather x1, waiting for transfers between devices, shards(): lax.all_gather(first_solved, 'row', axis=0, tiled=True)  68.8 us
    psum x1, blocking collectives, shards(): explained = lax.psum(partial_sums, 'row') / (2.0 * B)  38.4 us
    all_gather x1, waiting for transfers between devices, shards(): inverse_two = lax.all_gather(second_inverse, 'col', axis=1, tiled=True)  31 us
    all_gather x1, waiting for transfers between devices, shards(): link_rows = lax.all_gather(coupling, 'col', axis=1, tiled=True)  24.4 us
    dot_general x3, matrix products, product(): jnp.dot(left, right, precision=lax.Precision.HIGHEST, preferred_element_t...  22.5 us
    all_gather x1, waiting for transfers between devices, shards(): inverse_one = lax.all_gather(first_inverse, 'col', axis=1, tiled=True)  19.9 us
  transfers between devices with their start and end apart: 6, of which 6 were waited for; matrix products, arithmetic and copies ran while one was open for 9% of the time, Pallas kernels for 0%

commit v1 on v0

v1 whole, which is shorter than its diff:
```python
import jax
import jax.numpy as jnp
from jax import lax
from jax.experimental import pallas as pl
from jax.experimental.pallas import tpu as pltpu
from jax.sharding import PartitionSpec as P

W = 1960
B = 2048
CH = 128
Q = 6
PAIR = 2 * CH
MESH = pl.DeviceIdType.MESH
F32 = jnp.float32
BF16 = jnp.bfloat16

N_SEND = 640


def split(v):
    hi = v.astype(BF16)
    lo = (v - hi.astype(F32)).astype(BF16)
    return hi, lo


class Sent:
    def __init__(self, copy, number):
        self.copy = copy
        self.number = number


def task_order():
    tasks = []
    period, step = 13.0, 2.1
    base = 3.0
    for n in range(3):
        for q in range(Q):
            t = base + n * period + q * step
            if n == 0:
                t = base + q * 0.9
            for name, dt in (("b", 2.4), ("c", 4.6), ("d", 6.6), ("e", 9.0)):
                tt = t + dt
                if n == 0 and name in "cde":
                    tt = 10.0 + q * step + (dt - 4.6)
                tasks.append((tt, name, n, q))
    for k in range(5):
        tasks.append((2.0 + 1.9 * k, "ring", 0, k))
        tasks.append((8.4 + 2.2 * k, "ring", 1, k))
        tasks.append((18.5 + 2.4 * k, "ring", 2, k))
    tasks.append((9.9, "fac", 0, 0))
    tasks.append((17.8, "fac", 1, 0))
    tasks.append((28.9, "fac", 2, 0))
    for p in range(Q // 2):
        tasks.append((2.5 + 0.5 * p, "k1", 0, p))
        tasks.append((4.5 + 1.7 * p, "k2", 0, p))
    tasks.sort()
    return tasks


def kernel(desc_hbm, cand_hbm, f_hbm, c_hbm, s_hbm, first_out, second_out, ex_out,
           desc, cand, fin, fsend, fbuf, gbuf, pbuf, r1, r2, k2, esum, ebuf, lsem, ssem, rsem):
    row = lax.axis_index("row")
    col = lax.axis_index("col")
    x, y = row // 4, row % 4
    z, core = col // 2, col % 2
    counter = [0]
    sent = []

    def at(r, c):
        return {"row": r, "col": c}

    x_right, x_left = at(((x + 1) % 4) * 4 + y, col), at(((x + 3) % 4) * 4 + y, col)
    y_right, y_left = at(x * 4 + (y + 1) % 4, col), at(x * 4 + (y + 3) % 4, col)
    z_right, z_left = at(row, ((z + 1) % 8) * 2 + core), at(row, ((z + 7) % 8) * 2 + core)
    sibling = at(row, z * 2 + 1 - core)

    to_y = 2 * (z % 2) + core
    to_z = jnp.where(y < 2, z, z + 1 - 2 * (z % 2))
    from_z = (z // 2) * 2 + y // 2
    from_col = from_z * 2 + y % 2
    other_parity = (z % 2 + y // 2) % 2

    def new(src, dst, device):
        k = counter[0]
        counter[0] += 1
        return pltpu.make_async_remote_copy(
            src_ref=src, dst_ref=dst, send_sem=ssem.at[k], recv_sem=rsem.at[k],
            device_id=device, device_id_type=MESH)

    def send(src, dst, device):
        copy = new(src, dst, device)
        copy.start()
        sent.append(copy)
        return Sent(copy, counter[0] - 1)

    loads = []
    for m, ref in enumerate((f_hbm, c_hbm, s_hbm)):
        loads.append(pltpu.make_async_copy(ref, fin.at[m], lsem.at[m]))
    loads.append(pltpu.make_async_copy(desc_hbm, desc, lsem.at[3]))
    for p in range(Q // 2):
        columns = pl.ds(p * PAIR, PAIR)
        loads.append(pltpu.make_async_copy(cand_hbm.at[:, columns], cand.at[:, columns], lsem.at[4 + p]))
    for copy in loads:
        copy.start()

    barrier = pltpu.get_barrier_semaphore()
    partners = [at((row + d) % 16, col) for d in range(1, 16)] + [z_right, z_left, sibling]
    for i in range(2):
        partners.append(at(x * 4 + to_y, to_z * 2 + i))
        partners.append(at(x * 4 + 2 * other_parity + i, from_col))
    for device in partners:
        pl.semaphore_signal(barrier, inc=1, device_id=device, device_id_type=MESH)
    pl.semaphore_wait(barrier, len(partners))

    for m in range(3):
        loads[m].wait()
        hi, lo = split(fin[m])
        fsend[m, 0] = hi
        fsend[m, 1] = lo

    def rows_of(yi):
        return pl.ds(pl.multiple_of(yi * 128, 128), 128)

    def columns_of(zo):
        return pl.ds(pl.multiple_of((zo // 2) * 128, 128), 128)

    groups = ((0, 1), (1, 1), (2, 1))
    exchange = {}
    mine = (to_y == y) & (to_z == z)
    for g, (m0, count) in enumerate(groups):
        ms = pl.ds(m0, count)
        spot = (rows_of(y), columns_of(z))
        for c in range(2):
            k = counter[0]
            counter[0] += 2
            copy = pltpu.make_async_remote_copy(
                src_ref=fsend.at[ms, c], dst_ref=fbuf.at[ms, c, spot[0], spot[1]],
                send_sem=ssem.at[k], recv_sem=rsem.at[k + y % 2],
                device_id=at(x * 4 + to_y, to_z * 2 + c), device_id_type=MESH)
            local = mine & (core == c)
            exchange[g, c] = (copy, local, k)

            @pl.when(jnp.logical_not(local))
            def _(copy=copy):
                copy.start()

            @pl.when(local)
            def _(m0=m0, count=count, c=c, spot=spot):
                for m in range(m0, m0 + count):
                    fbuf[m, c, spot[0], spot[1]] = fsend[m, c]

    def wait_exchange(g):
        m0, count = groups[g]
        ms = pl.ds(m0, count)
        for c in range(2):
            _, _, k = exchange[g, c]
            for i in range(2):
                yi = 2 * other_parity + i
                local = (yi == y) & (from_col == col)
                spot = fbuf.at[ms, c, rows_of(yi), columns_of(z)]
                arrival = pltpu.make_async_remote_copy(
                    src_ref=spot, dst_ref=spot, send_sem=ssem.at[k], recv_sem=rsem.at[k + i],
                    device_id=sibling, device_id_type=MESH)

                @pl.when((core == c) & jnp.logical_not(local))
                def _(arrival=arrival):
                    arrival.wait_recv()

    def piece(g, h, zo, half=None):
        m0, count = groups[g]
        other = (zo % 2 + y // 2) % 2
        start, size = other * 256, 256
        if half is not None:
            start, size = start + half * 128, 128
        return fbuf.at[pl.ds(m0, count), h, pl.ds(pl.multiple_of(start, 128), size), columns_of(zo)]

    ring_sends = {}
    sibling_sends = {0: [], 1: [], 2: []}

    def ring(g, k):
        h = core
        right_zo, left_zo = (z + 8 - k) % 8, (z + k) % 8
        if k == 0:
            wait_exchange(g)
            own = piece(g, h, z)
            ring_sends[g, 1] = (send(own, own, z_right), send(own, own, z_left))
            sibling_sends[g].append((send(own, own, sibling), z, None))
            return
        for side, zo in ((0, right_zo), (1, left_zo)):
            half = None if k < 4 else side
            got = piece(g, h, zo, half)
            arrival = ring_sends[g, k][side]
            pltpu.make_async_remote_copy(
                src_ref=got, dst_ref=got, send_sem=ssem.at[arrival.number], recv_sem=rsem.at[arrival.number],
                device_id=sibling, device_id_type=MESH).wait_recv()
            if k < 4:
                out = got if k < 3 else piece(g, h, zo, side)
                onward = send(out, out, z_right if side == 0 else z_left)
                ring_sends.setdefault((g, k + 1), []).append(onward)
            sibling_sends[g].append((send(got, got, sibling), zo, half))

    def factors_ready(g):
        for copy, zo, half in sibling_sends[g]:
            got = piece(g, 1 - core, zo, half)
            pltpu.make_async_remote_copy(
                src_ref=got, dst_ref=got, send_sem=ssem.at[copy.number], recv_sem=rsem.at[copy.number],
                device_id=sibling, device_id_type=MESH).wait_recv()

    def block_of(i):
        return pl.ds(pl.multiple_of((i % 4) * 128, 128), 128)

    def half_of(i, half):
        return pl.ds(pl.multiple_of((i % 4) * 128 + half * 64, 64), 64)

    def wait_recv(copy, ref):
        pltpu.make_async_remote_copy(
            src_ref=ref, dst_ref=ref, send_sem=ssem.at[copy.number], recv_sem=rsem.at[copy.number],
            device_id=sibling, device_id_type=MESH).wait_recv()

    state = {}

    def put(n, q, v):
        hi, lo = split(v)
        gbuf[n, q, block_of(x), 0:CH] = hi
        gbuf[n, q, block_of(x), CH:PAIR] = lo
        own = gbuf.at[n, q, block_of(x)]
        state["a", n, q] = (send(own, own, x_right), send(own, own, x_left))

    def kernel_columns(panel, p):
        inner = lax.dot_general(
            desc[panel], cand[:, p * PAIR:(p + 1) * PAIR], (((0,), (0,)), ((), ())),
            preferred_element_type=F32)
        return inner * inner

    def k1_task(p):
        if p == 0:
            loads[3].wait()
        loads[4 + p].wait()
        value = kernel_columns(0, p)
        for i in range(2):
            put(0, 2 * p + i, value[:, i * CH:(i + 1) * CH])

    def k2_task(p):
        value = kernel_columns(1, p)
        for i in range(2):
            k2[2 * p + i] = value[:, i * CH:(i + 1) * CH]

    def b_task(n, q):
        to_right, to_left = state["a", n, q]
        wait_recv(to_right, gbuf.at[n, q, block_of(x + 3)])
        top = gbuf.at[n, q, half_of(x + 3, 0)]
        on_right = send(top, top, x_right)
        wait_recv(to_left, gbuf.at[n, q, block_of(x + 1)])
        bottom = gbuf.at[n, q, half_of(x + 1, 1)]
        on_left = send(bottom, bottom, x_left)
        state["b", n, q] = (on_right, on_left)

    def c_task(n, q):
        on_right, on_left = state["b", n, q]
        wait_recv(on_right, gbuf.at[n, q, half_of(x + 2, 0)])
        wait_recv(on_left, gbuf.at[n, q, half_of(x + 2, 1)])
        v = gbuf[n, q]
        v_hi = v[:, 0:CH]
        for i in range(2):
            rows = slice(i * 256, (i + 1) * 256)
            both = jnp.dot(fbuf[n, 0, rows, :], v, preferred_element_type=F32)
            low = jnp.dot(fbuf[n, 1, rows, :], v_hi, preferred_element_type=F32)
            pbuf[n, q, rows, :] = both[:, 0:CH] + (both[:, CH:PAIR] + low)
        copies = (
            send(pbuf.at[n, q, half_of(y + 2, 0)], r1.at[n, q, 0], y_right),
            send(pbuf.at[n, q, half_of(y + 2, 1)], r1.at[n, q, 1], y_left),
            send(pbuf.at[n, q, half_of(y + 1, 1)], r2.at[n, q, 0, pl.ds(64, 64)], y_right),
            send(pbuf.at[n, q, half_of(y + 3, 0)], r2.at[n, q, 1, pl.ds(0, 64)], y_left),
        )
        state["c", n, q] = copies

    def d_task(n, q):
        copies = state["c", n, q]
        wait_recv(copies[0], r1.at[n, q, 0])
        rows = half_of(y + 1, 0)
        pbuf[n, q, rows, :] = pbuf[n, q, rows, :] + r1[n, q, 0]
        right = send(pbuf.at[n, q, rows], r2.at[n, q, 0, pl.ds(0, 64)], y_right)
        wait_recv(copies[1], r1.at[n, q, 1])
        rows = half_of(y + 3, 1)
        pbuf[n, q, rows, :] = pbuf[n, q, rows, :] + r1[n, q, 1]
        left = send(pbuf.at[n, q, rows], r2.at[n, q, 1, pl.ds(64, 64)], y_left)
        state["d", n, q] = (right, left)

    def e_task(n, q):
        copies = state["c", n, q]
        right, left = state["d", n, q]
        wait_recv(copies[2], r2.at[n, q, 0, pl.ds(64, 64)])
        wait_recv(copies[3], r2.at[n, q, 1, pl.ds(0, 64)])
        wait_recv(right, r2.at[n, q, 0, pl.ds(0, 64)])
        wait_recv(left, r2.at[n, q, 1, pl.ds(64, 64)])
        value = pbuf[n, q, block_of(y), :] + (r2[n, q, 0] + r2[n, q, 1])
        columns = slice(q * CH, (q + 1) * CH)
        if n == 0:
            put(1, q, value)
            first_out[:, columns] = value
            esum[q:q + 1, :] = jnp.sum(value * value, axis=0, keepdims=True)
        elif n == 1:
            put(2, q, k2[q] - value)
        else:
            esum[q:q + 1, :] = esum[q:q + 1, :] + jnp.sum(value * value, axis=0, keepdims=True)
            second_out[:, columns] = value

    esum[...] = jnp.zeros_like(esum)
    for _, name, n, q in task_order():
        if name == "ring":
            ring(n, q)
        elif name == "fac":
            factors_ready(n)
        elif name == "k1":
            k1_task(q)
        elif name == "k2":
            k2_task(q)
        else:
            {"b": b_task, "c": c_task, "d": d_task, "e": e_task}[name](n, q)

    ebuf[pl.ds(row, 1)] = esum[...][None]
    spread = []
    for d in range(1, 16):
        spread.append(send(esum, ebuf.at[row], at((row + d) % 16, col)))
    for d in range(1, 16):
        wait_recv(spread[d - 1], ebuf.at[(row + 16 - d) % 16])
    total = ebuf[0]
    for i in range(1, 16):
        total = total + ebuf[i]
    ex_out[...] = total * (1.0 / (2.0 * B))

    for copy in sent:
        copy.wait_send()
    for copy, local, _ in exchange.values():
        @pl.when(jnp.logical_not(local))
        def _(copy=copy):
            copy.wait_send()
    assert counter[0] <= N_SEND


def shards(inducing_desc, candidate_desc, first_inverse, coupling, second_inverse):
    hbm = pl.BlockSpec(memory_space=pl.ANY)
    vmem = pl.BlockSpec(memory_space=pltpu.VMEM)
    first, second, explained = pl.pallas_call(
        kernel,
        out_shape=(
            jax.ShapeDtypeStruct((128, Q * CH), F32),
            jax.ShapeDtypeStruct((128, Q * CH), F32),
            jax.ShapeDtypeStruct((8, 128), F32),
        ),
        in_specs=[hbm] * 5,
        out_specs=(vmem, vmem, vmem),
        scratch_shapes=[
            pltpu.VMEM((2, W, 128), BF16),
            pltpu.VMEM((W, Q * CH), BF16),
            pltpu.VMEM((3, 128, 128), F32),
            pltpu.VMEM((3, 2, 128, 128), BF16),
            pltpu.VMEM((3, 2, 512, 512), BF16),
            pltpu.VMEM((3, Q, 512, PAIR), BF16),
            pltpu.VMEM((3, Q, 512, CH), F32),
            pltpu.VMEM((3, Q, 2, 64, CH), F32),
            pltpu.VMEM((3, Q, 2, 128, CH), F32),
            pltpu.VMEM((Q, 128, CH), F32),
            pltpu.VMEM((8, 128), F32),
            pltpu.VMEM((16, 8, 128), F32),
            pltpu.SemaphoreType.DMA((4 + Q // 2,)),
            pltpu.SemaphoreType.DMA((N_SEND,)),
            pltpu.SemaphoreType.DMA((N_SEND,)),
        ],
        compiler_params=pltpu.CompilerParams(
            collective_id=0, has_side_effects=True, vmem_limit_bytes=48 * 1024 * 1024),
    )(inducing_desc, candidate_desc, first_inverse, coupling, second_inverse)
    return first, second, explained[:Q].reshape(Q * CH)


def solution(mesh):
    return jax.shard_map(
        shards,
        mesh=mesh,
        in_specs=(
            P(None, None, "row"),
            P(None, "col"),
            P("row", "col"),
            P("row", "col"),
            P("row", "col"),
        ),
        out_specs=(P("row", "col"), P("row", "col"), P("col")),
        check_vma=False,
    )
```

time: 442 us -> 130 us (0.29)
  waiting for transfers between devices: 342 us -> 0 us
  Pallas kernels: 0 us -> 121 us
  matrix products: 41 us -> 0 us
  blocking collectives: 38.4 us -> 0 us
  between operations: 14.1 us -> 0.65 us
    all_gather x6 -> x0, waiting for transfers between devices: 339 us -> none  [the longest x1 126 us: shards(): lax.all_gather(inducing_desc, 'row', axis=2, tiled=True)]
    pallas_call x0 -> x1, Pallas kernels: none -> 121 us  [shards(): pl.pallas_call(kernel, out_shape=(jax.ShapeDtypeStruct((128, Q * CH), F32...]
    dot_general x4 -> x0, matrix products: 41 us -> none  [the longest x3 22.5 us: product(): jnp.dot(left, right, precision=lax.Precision.HIGHEST, preferred_element_t...]
    psum x1 -> x0, blocking collectives: 38.4 us -> none  [shards(): explained = lax.psum(partial_sums, 'row') / (2.0 * B)]
    unnamed x2 -> x12, local copies, waits for them, and re-layouts: 0.01 us -> 7.06 us
    slice x1 -> x0, local copies, waits for them, and re-layouts: 5.83 us -> none  [shards(): second_kernel = lax.dynamic_slice_in_dim(kernels[1], begin, share, 0)]
  transfers between devices with their start and end apart: 6 -> 0, of which waited for: 6 -> 0; matrix products, arithmetic and copies ran while one was open for 9% -> 0% of each run, Pallas kernels for 0% -> 0%
where the time goes in v1:
time: 130 us; the launch traced here: 129 us
  Pallas kernels  121 us (93%)
  local copies, waits for them, and re-layouts  7.66 us (6%)
    pallas_call x1, Pallas kernels, shards(): pl.pallas_call(kernel, out_shape=(jax.ShapeDtypeStruct((128, Q * CH), F32...  121 us
    unnamed x12, local copies, waits for them, and re-layouts  7.06 us

profile of v1, /device:TPU:32, one launch (start us, length us, event | category | flops | bytes accessed | tf_op | source)
XLA Modules:
  0.0 129.2 jit_solution(5284211821696879281)
XLA Ops:
  0.6 0.0 copy-start
  0.6 1.8 %copy-done = bf16[1960,768]{1,0:T(8,128)(2,1)S(1)} copy-done((bf16[1960,768]{1,0:T(8,128)(2,1)S(1)}, bf16[1960,768]{1,0:T(8,128)(2,1)}, u32[]{:S(2)}) %copy-start) | copy-done | bytes 3010584
  2.5 0.0 copy-start.1
  2.5 1.2 copy-done.1
  3.7 0.0 copy-start.2
  3.7 0.8 copy-done.2
  4.5 0.0 copy-start.3
  4.5 0.8 copy-done.3
  5.4 0.0 copy-start.4
  5.4 0.8 copy-done.4
  6.2 120.9 %shard_map.76 = (f32[128,768]{1,0:T(8,128)S(1)}, f32[128,768]{1,0:T(8,128)S(1)}, f32[8,128]{1,0:T(8,128)S(1)}) custom-call(bf16[2,1960,128]{2,1,0:T(8,128)(2,1)S(1)} %copy-done.1, bf16[1960,768]{1,0:T(8,128)(2,1)S(1)} %copy-done, f32[128,128]{1,0:T(8,128)S(1)} %copy-done.2, f32[128,128]{1,0:T(8,128)S(1)} %copy-done.3, f32[128,128]{1,0:T(8,128)S(1)} %copy-done.4), custom_call_target="tpu_custom_call" | custom-call | tf_op jit(solution)/shard_map/pallas_call | solution.py:344
  127.2 0.6 slice_bitcast_fusion
  127.8 0.7 copy.10
  128.5 0.7 copy.11
Async XLA Ops:
  0.6 1.9 %copy-start = (bf16[1960,768]{1,0:T(8,128)(2,1)S(1)}, bf16[1960,768]{1,0:T(8,128)(2,1)}, u32[]{:S(2)}) copy-start(bf16[1960,768]{1,0:T(8,128)(2,1)} %cand_hbm.1) | copy-start | bytes 9031684
  2.5 1.2 copy-start.1
  3.7 0.8 copy-start.2
  4.5 0.8 copy-start.3
  5.4 0.8 copy-start.4

commit v2 on v0

v2 whole, which is shorter than its diff:
```python
import jax
import jax.numpy as jnp
from jax import lax
from jax.experimental import pallas as pl
from jax.experimental.pallas import tpu as pltpu
from jax.sharding import PartitionSpec as P

W = 1960
B = 2048
CH = 128
Q = 6
PAIR = 2 * CH
MESH = pl.DeviceIdType.MESH
F32 = jnp.float32
BF16 = jnp.bfloat16

N_SEND = 256
ROWS = 144
TINY = 1e-35


def split(v):
    hi = v.astype(BF16)
    lo = (v - hi.astype(F32)).astype(BF16)
    return hi, lo


def encode(ref, v, diagonal=None):
    top = jnp.max(jnp.abs(v), axis=0, keepdims=True)
    s = (top * 1.01 + TINY).astype(BF16)
    t = jnp.abs(v) * (250.0 / s.astype(F32))
    e = jnp.floor(t)
    c = jnp.exp2(e - 125.0) * ((t - e) + 1.0)
    ref[0:128, :] = jnp.where(v < 0.0, -c, c).astype(BF16)
    tail = jnp.broadcast_to(s.astype(F32), (16, 128))
    if diagonal is not None:
        hi, lo = split(diagonal)
        index = lax.broadcasted_iota(jnp.int32, (16, 128), 0)
        tail = jnp.where(index == 1, hi.astype(F32), jnp.where(index == 2, lo.astype(F32), tail))
    ref[128:144, :] = tail.astype(BF16)


def decode(ref):
    c = ref[0:128, :].astype(F32)
    tail = ref[128:144, :].astype(F32)
    a = jnp.abs(c)
    e = jnp.floor(jnp.log2(a) + 0.002)
    t = (e + (a * jnp.exp2(-e) + 124.0)) * (tail[0:1, :] * (1.0 / 250.0))
    return jnp.where(c < 0.0, -t, t), tail[1:2, :] + tail[2:3, :]


class Sent:
    def __init__(self, copy, number):
        self.copy = copy
        self.number = number


def task_order():
    tasks = []
    start, period, step, flight = 14.0, 10.6, 1.65, 5.2
    for n in range(3):
        for q in range(Q):
            t = start + n * period + q * step
            tasks.append((t, "c", n, q))
            tasks.append((t + flight, "e", n, q))
    for p in range(Q // 2):
        tasks.append((3.0 + 0.5 * p, "k1", 0, p))
        tasks.append((5.0 + 0.5 * p, "k2", 0, p))
    for m in range(3):
        tasks.append(((2.0, 7.0, 13.0)[m], "fsend", m, 0))
        tasks.append(((10.0, 16.0, 24.0)[m], "sibling", m, 0))
        tasks.append(((13.9, 20.0, 30.0)[m], "fac", m, 0))
    tasks.sort()
    return tasks


def kernel(desc_hbm, cand_hbm, f_hbm, c_hbm, s_hbm, first_out, second_out, ex_out,
           desc, cand, fin, fmsg, frecv, fbuf, vown, vsend, vrecv, gbuf, pown, ptmp, psend, precv,
           k2, esum, ebuf, lsem, ssem, rsem):
    row = lax.axis_index("row")
    col = lax.axis_index("col")
    x, y = row // 4, row % 4
    z, core = col // 2, col % 2
    counter = [0]
    sent = []

    def at(r, c):
        return {"row": r, "col": c}

    sibling = at(row, z * 2 + 1 - core)
    to_y = 2 * (z % 2) + core
    parity = y % 2

    def take(count=1):
        k = counter[0]
        counter[0] += count
        return k

    def send(src, dst, device):
        k = take()
        copy = pltpu.make_async_remote_copy(
            src_ref=src, dst_ref=dst, send_sem=ssem.at[k], recv_sem=rsem.at[k],
            device_id=device, device_id_type=MESH)
        copy.start()
        sent.append(copy)
        return k

    def arrival(k, ref):
        return pltpu.make_async_remote_copy(
            src_ref=ref, dst_ref=ref, send_sem=ssem.at[k], recv_sem=rsem.at[k],
            device_id=sibling, device_id_type=MESH)

    loads = []
    for m, ref in enumerate((f_hbm, c_hbm, s_hbm)):
        loads.append(pltpu.make_async_copy(ref, fin.at[m], lsem.at[m]))
    loads.append(pltpu.make_async_copy(desc_hbm, desc, lsem.at[3]))
    for p in range(Q // 2):
        columns = pl.ds(p * PAIR, PAIR)
        loads.append(pltpu.make_async_copy(cand_hbm.at[:, columns], cand.at[:, columns], lsem.at[4 + p]))
    for copy in loads:
        copy.start()

    barrier = pltpu.get_barrier_semaphore()
    partners = [at((row + d) % 16, col) for d in range(1, 16)] + [sibling]
    for i in range(8):
        partners.append(at(x * 4 + to_y, i * 2 + parity))
    for i in range(4):
        for j in range(2):
            partners.append(at(x * 4 + 2 * j + core, (2 * i + y // 2) * 2 + parity))
    for device in partners:
        pl.semaphore_signal(barrier, inc=1, device_id=device, device_id_type=MESH)

    eye = lax.broadcasted_iota(jnp.int32, (128, 128), 0) == lax.broadcasted_iota(jnp.int32, (128, 128), 1)
    on_diagonal = row == col
    factor_sends = {}
    factor_base = {}

    def encode_factor(m):
        loads[m].wait()
        block = fin[m]
        if m == 1:
            encode(fmsg.at[m], block, jnp.zeros((1, 128), F32))
        else:
            taken = eye & on_diagonal
            diagonal = jnp.sum(jnp.where(taken, block, 0.0), axis=0, keepdims=True)
            encode(fmsg.at[m], jnp.where(taken, 0.0, block), diagonal)

    def fsend_task(m):
        base = take(8)
        factor_base[m] = base
        slot = frecv.at[m, parity, z // 2, y // 2]
        for i, dz in enumerate((4, 3, 5, 2, 6, 1, 7, 0)):
            copy = pltpu.make_async_remote_copy(
                src_ref=fmsg.at[m], dst_ref=slot, send_sem=ssem.at[base + i],
                recv_sem=rsem.at[base + (z // 2) * 2 + y // 2],
                device_id=at(x * 4 + to_y, ((z + dz) % 8) * 2 + parity), device_id_type=MESH)
            if dz:
                copy.start()
                sent.append(copy)
            else:
                local = (to_y == y) & (core == parity)
                factor_sends[m] = (copy, local)

                @pl.when(jnp.logical_not(local))
                def _(copy=copy):
                    copy.start()

                @pl.when(local)
                def _():
                    frecv[m, parity, z // 2, y // 2] = fmsg[m]

    sibling_copy = {}

    def sibling_task(m):
        for i in range(4):
            for j in range(2):
                got = arrival(factor_base[m] + 2 * i + j, frecv.at[m, core, i, j])
                mine = (2 * j + core == y) & (2 * i + y // 2 == z) & (parity == core)

                @pl.when(jnp.logical_not(mine))
                def _(got=got):
                    got.wait_recv()
        sibling_copy[m] = send(frecv.at[m, core], frecv.at[m, core], sibling)

    def fac_task(m):
        arrival(sibling_copy[m], frecv.at[m, 1 - core]).wait_recv()
        for p in range(2):
            for i in range(4):
                for j in range(2):
                    value, diagonal = decode(frecv.at[m, p, i, j])
                    if m != 1:
                        value = value + jnp.where(eye, diagonal, 0.0)
                    hi, lo = split(value)
                    r = (2 * j + p) * 128
                    fbuf[m, 0, r:r + 128, i * 128:(i + 1) * 128] = hi
                    fbuf[m, 1, r:r + 128, i * 128:(i + 1) * 128] = lo

    def block_of(i):
        return pl.ds(pl.multiple_of((i % 4) * 128, 128), 128)

    gathers = {}
    scatters = {}

    def put(n, q, v):
        vown[n, q] = v
        encode(vsend.at[n, q], v)
        gathers[n, q] = [
            send(vsend.at[n, q], vrecv.at[n, q, d - 1], at(((x + 4 - d) % 4) * 4 + y, col))
            for d in (2, 1, 3)]

    def kernel_columns(panel, p):
        inner = lax.dot_general(
            desc[panel], cand[:, p * PAIR:(p + 1) * PAIR], (((0,), (0,)), ((), ())),
            preferred_element_type=F32)
        return inner * inner

    def k1_task(p):
        if p == 0:
            loads[3].wait()
        loads[4 + p].wait()
        value = kernel_columns(0, p)
        for i in range(2):
            put(0, 2 * p + i, value[:, i * CH:(i + 1) * CH])

    def k2_task(p):
        value = kernel_columns(1, p)
        for i in range(2):
            k2[2 * p + i] = value[:, i * CH:(i + 1) * CH]

    def c_task(n, q):
        hi, lo = split(vown[n, q])
        gbuf[block_of(x), 0:CH] = hi
        gbuf[block_of(x), CH:PAIR] = lo
        for k, d in zip(gathers[n, q], (2, 1, 3)):
            arrival(k, vrecv.at[n, q, d - 1]).wait_recv()
        for d in (1, 2, 3):
            value, _ = decode(vrecv.at[n, q, d - 1])
            hi, lo = split(value)
            gbuf[block_of(x + d), 0:CH] = hi
            gbuf[block_of(x + d), CH:PAIR] = lo
        v = gbuf[...]
        v_hi = v[:, 0:CH]
        for i in range(2):
            rows = slice(i * 256, (i + 1) * 256)
            both = jnp.dot(fbuf[n, 0, rows, :], v, preferred_element_type=F32)
            low = jnp.dot(fbuf[n, 1, rows, :], v_hi, preferred_element_type=F32)
            ptmp[rows, :] = both[:, 0:CH] + (both[:, CH:PAIR] + low)
        ks = []
        for d in (2, 1, 3):
            encode(psend.at[n, q, d - 1], ptmp[block_of(y + 4 - d), :])
            ks.append(send(psend.at[n, q, d - 1], precv.at[n, q, d - 1], at(x * 4 + (y + 4 - d) % 4, col)))
        scatters[n, q] = ks
        pown[n, q] = ptmp[block_of(y), :]

    def e_task(n, q):
        for k, d in zip(scatters[n, q], (2, 1, 3)):
            arrival(k, precv.at[n, q, d - 1]).wait_recv()
        value = pown[n, q]
        for d in (1, 2, 3):
            value = value + decode(precv.at[n, q, d - 1])[0]
        columns = slice(q * CH, (q + 1) * CH)
        if n == 0:
            put(1, q, value)
            first_out[:, columns] = value
            esum[q:q + 1, :] = jnp.sum(value * value, axis=0, keepdims=True)
        elif n == 1:
            put(2, q, k2[q] - value)
        else:
            esum[q:q + 1, :] = esum[q:q + 1, :] + jnp.sum(value * value, axis=0, keepdims=True)
            second_out[:, columns] = value

    esum[...] = jnp.zeros_like(esum)
    for m in range(3):
        encode_factor(m)
    pl.semaphore_wait(barrier, len(partners))
    for _, name, n, q in task_order():
        if name == "fsend":
            fsend_task(n)
        elif name == "sibling":
            sibling_task(n)
        elif name == "fac":
            fac_task(n)
        elif name == "k1":
            k1_task(q)
        elif name == "k2":
            k2_task(q)
        elif name == "c":
            c_task(n, q)
        else:
            e_task(n, q)

    ebuf[pl.ds(row, 1)] = esum[...][None]
    spread = [send(esum, ebuf.at[row], at((row + d) % 16, col)) for d in range(1, 16)]
    for d in range(1, 16):
        arrival(spread[d - 1], ebuf.at[(row + 16 - d) % 16]).wait_recv()
    total = ebuf[0]
    for i in range(1, 16):
        total = total + ebuf[i]
    ex_out[...] = total * (1.0 / (2.0 * B))

    for copy in sent:
        copy.wait_send()
    for copy, local in factor_sends.values():
        @pl.when(jnp.logical_not(local))
        def _(copy=copy):
            copy.wait_send()
    assert counter[0] <= N_SEND


def shards(inducing_desc, candidate_desc, first_inverse, coupling, second_inverse):
    hbm = pl.BlockSpec(memory_space=pl.ANY)
    vmem = pl.BlockSpec(memory_space=pltpu.VMEM)
    first, second, explained = pl.pallas_call(
        kernel,
        out_shape=(
            jax.ShapeDtypeStruct((128, Q * CH), F32),
            jax.ShapeDtypeStruct((128, Q * CH), F32),
            jax.ShapeDtypeStruct((8, 128), F32),
        ),
        in_specs=[hbm] * 5,
        out_specs=(vmem, vmem, vmem),
        scratch_shapes=[
            pltpu.VMEM((2, W, 128), BF16),
            pltpu.VMEM((W, Q * CH), BF16),
            pltpu.VMEM((3, 128, 128), F32),
            pltpu.VMEM((3, ROWS, 128), BF16),
            pltpu.VMEM((3, 2, 4, 2, ROWS, 128), BF16),
            pltpu.VMEM((3, 2, 512, 512), BF16),
            pltpu.VMEM((3, Q, 128, CH), F32),
            pltpu.VMEM((3, Q, ROWS, CH), BF16),
            pltpu.VMEM((3, Q, 3, ROWS, CH), BF16),
            pltpu.VMEM((512, PAIR), BF16),
            pltpu.VMEM((3, Q, 128, CH), F32),
            pltpu.VMEM((512, CH), F32),
            pltpu.VMEM((3, Q, 3, ROWS, CH), BF16),
            pltpu.VMEM((3, Q, 3, ROWS, CH), BF16),
            pltpu.VMEM((Q, 128, CH), F32),
            pltpu.VMEM((8, 128), F32),
            pltpu.VMEM((16, 8, 128), F32),
            pltpu.SemaphoreType.DMA((4 + Q // 2,)),
            pltpu.SemaphoreType.DMA((N_SEND,)),
            pltpu.SemaphoreType.DMA((N_SEND,)),
        ],
        compiler_params=pltpu.CompilerParams(
            collective_id=0, has_side_effects=True, vmem_limit_bytes=60 * 1024 * 1024),
    )(inducing_desc, candidate_desc, first_inverse, coupling, second_inverse)
    return first, second, explained[:Q].reshape(Q * CH)


def solution(mesh):
    return jax.shard_map(
        shards,
        mesh=mesh,
        in_specs=(
            P(None, None, "row"),
            P(None, "col"),
            P("row", "col"),
            P("row", "col"),
            P("row", "col"),
        ),
        out_specs=(P("row", "col"), P("row", "col"), P("col")),
        check_vma=False,
    )
```

time: 442 us -> 75.1 us (0.17)
  waiting for transfers between devices: 342 us -> 0 us
  Pallas kernels: 0 us -> 68.8 us
  matrix products: 41 us -> 0 us
  blocking collectives: 38.4 us -> 0 us
  between operations: 14.1 us -> 0.64 us
    all_gather x6 -> x0, waiting for transfers between devices: 339 us -> none  [the longest x1 126 us: shards(): lax.all_gather(inducing_desc, 'row', axis=2, tiled=True)]
    pallas_call x0 -> x1, Pallas kernels: none -> 68.8 us  [shards(): pl.pallas_call(kernel, out_shape=(jax.ShapeDtypeStruct((128, Q * CH), F32...]
    dot_general x4 -> x0, matrix products: 41 us -> none  [the longest x3 22.5 us: product(): jnp.dot(left, right, precision=lax.Precision.HIGHEST, preferred_element_t...]
    psum x1 -> x0, blocking collectives: 38.4 us -> none  [shards(): explained = lax.psum(partial_sums, 'row') / (2.0 * B)]
    slice x1 -> x0, local copies, waits for them, and re-layouts: 5.83 us -> none  [shards(): second_kernel = lax.dynamic_slice_in_dim(kernels[1], begin, share, 0)]
  transfers between devices with their start and end apart: 6 -> 0, of which waited for: 6 -> 0; matrix products, arithmetic and copies ran while one was open for 9% -> 0% of each run, Pallas kernels for 0% -> 0%
where the time goes in v2:
time: 75.1 us; the launch traced here: 74.3 us
  Pallas kernels  68.8 us (92%)
  local copies, waits for them, and re-layouts  4.8 us (6%)
    pallas_call x1, Pallas kernels, shards(): pl.pallas_call(kernel, out_shape=(jax.ShapeDtypeStruct((128, Q * CH), F32...  68.8 us
    unnamed x2, local copies, waits for them, and re-layouts  3.53 us

profile of v2, /device:TPU:32, one launch (start us, length us, event | category | flops | bytes accessed | tf_op | source)
XLA Modules:
  0.0 74.3 jit_solution(15920567722598329990)
XLA Ops:
  0.6 68.8 %shard_map.76 = (f32[128,768]{1,0:T(8,128)}, f32[128,768]{1,0:T(8,128)}, f32[8,128]{1,0:T(8,128)}) custom-call(bf16[2,1960,128]{2,1,0:T(8,128)(2,1)} %desc_hbm.1, bf16[1960,768]{1,0:T(8,128)(2,1)} %cand_hbm.1, f32[128,128]{1,0:T(8,128)} %f_hbm.1, f32[128,128]{1,0:T(8,128)} %c_hbm.1, f32[128,128]{1,0:T(8,128)} %s_hbm.1), custom_call_target="tpu_custom_call" | custom-call | tf_op jit(solution)/shard_map/pallas_call | solution.py:313
  69.5 1.3 %slice_bitcast_fusion = f32[768]{0:T(1024)} fusion(f32[8,128]{1,0:T(8,128)} %get-tuple-element.8), kind=kLoop, calls=%fused_computation | loop fusion | bytes 6144 | tf_op jit(solution)/shard_map/reshape | solution.py:347
  70.7 1.8 %copy.10 = f32[128,768]{1,0:T(8,128)} copy(f32[128,768]{1,0:T(8,128)} %get-tuple-element.12) | data formatting | bytes 786432
  72.5 1.8 %copy.11 = f32[128,768]{1,0:T(8,128)} copy(f32[128,768]{1,0:T(8,128)} %get-tuple-element.13) | data formatting | bytes 786432

commit v3 on v2

--- a/solution.py
+++ b/solution.py
@@ -14,7 +14,8 @@
 F32 = jnp.float32
 BF16 = jnp.bfloat16
 
-N_SEND = 256
+GATHER, SCATTER, FACTOR, SIBLING, SPREAD, N_RECV = 0, 18, 36, 39, 42, 43
+GATHER_OUT, SCATTER_OUT, FACTOR_OUT, SIBLING_OUT, SPREAD_OUT, N_SEND = 0, 1, 2, 5, 8, 9
 ROWS = 144
 TINY = 1e-35
 
@@ -47,12 +48,6 @@
     e = jnp.floor(jnp.log2(a) + 0.002)
     t = (e + (a * jnp.exp2(-e) + 124.0)) * (tail[0:1, :] * (1.0 / 250.0))
     return jnp.where(c < 0.0, -t, t), tail[1:2, :] + tail[2:3, :]
-
-
-class Sent:
-    def __init__(self, copy, number):
-        self.copy = copy
-        self.number = number
 
 
 def task_order():
@@ -81,8 +76,6 @@
     col = lax.axis_index("col")
     x, y = row // 4, row % 4
     z, core = col // 2, col % 2
-    counter = [0]
-    sent = []
 
     def at(r, c):
         return {"row": r, "col": c}
@@ -91,24 +84,16 @@
     to_y = 2 * (z % 2) + core
     parity = y % 2
 
-    def take(count=1):
-        k = counter[0]
-        counter[0] += count
-        return k
-
-    def send(src, dst, device):
-        k = take()
-        copy = pltpu.make_async_remote_copy(
-            src_ref=src, dst_ref=dst, send_sem=ssem.at[k], recv_sem=rsem.at[k],
+    def remote(src, dst, out, into, device):
+        return pltpu.make_async_remote_copy(
+            src_ref=src, dst_ref=dst, send_sem=ssem.at[out], recv_sem=rsem.at[into],
             device_id=device, device_id_type=MESH)
-        copy.start()
-        sent.append(copy)
-        return k
-
-    def arrival(k, ref):
-        return pltpu.make_async_remote_copy(
-            src_ref=ref, dst_ref=ref, send_sem=ssem.at[k], recv_sem=rsem.at[k],
-            device_id=sibling, device_id_type=MESH)
+
+    def arrived(into, ref):
+        remote(ref, ref, 0, into, sibling).wait_recv()
+
+    def departed(out, ref):
+        remote(ref, ref, out, 0, sibling).wait_send()
 
     loads = []
     for m, ref in enumerate((f_hbm, c_hbm, s_hbm)):
@@ -122,8 +107,6 @@
 
     barrier = pltpu.get_barrier_semaphore()
     partners = [at((row + d) % 16, col) for d in range(1, 16)] + [sibling]
-    for i in range(8):
-        partners.append(at(x * 4 + to_y, i * 2 + parity))
     for i in range(4):
         for j in range(2):
             partners.append(at(x * 4 + 2 * j + core, (2 * i + y // 2) * 2 + parity))
@@ -132,9 +115,6 @@
 
     eye = lax.broadcasted_iota(jnp.int32, (128, 128), 0) == lax.broadcasted_iota(jnp.int32, (128, 128), 1)
     on_diagonal = row == col
-    factor_sends = {}
-    factor_base = {}
-
     def encode_factor(m):
         loads[m].wait()
         block = fin[m]
@@ -145,49 +125,35 @@
             diagonal = jnp.sum(jnp.where(taken, block, 0.0), axis=0, keepdims=True)
             encode(fmsg.at[m], jnp.where(taken, 0.0, block), diagonal)
 
+    here = (to_y == y) & (core == parity)
+    my_slot = pl.ds(pl.multiple_of(((z // 2) * 2 + y // 2) * ROWS, 16), ROWS)
+
     def fsend_task(m):
-        base = take(8)
-        factor_base[m] = base
-        slot = frecv.at[m, parity, z // 2, y // 2]
-        for i, dz in enumerate((4, 3, 5, 2, 6, 1, 7, 0)):
-            copy = pltpu.make_async_remote_copy(
-                src_ref=fmsg.at[m], dst_ref=slot, send_sem=ssem.at[base + i],
-                recv_sem=rsem.at[base + (z // 2) * 2 + y // 2],
-                device_id=at(x * 4 + to_y, ((z + dz) % 8) * 2 + parity), device_id_type=MESH)
+        slot = frecv.at[m, parity, my_slot]
+        for dz in (4, 3, 5, 2, 6, 1, 7, 0):
+            copy = remote(fmsg.at[m], slot, FACTOR_OUT + m, FACTOR + m,
+                          at(x * 4 + to_y, ((z + dz) % 8) * 2 + parity))
             if dz:
                 copy.start()
-                sent.append(copy)
             else:
-                local = (to_y == y) & (core == parity)
-                factor_sends[m] = (copy, local)
-
-                @pl.when(jnp.logical_not(local))
-                def _(copy=copy):
+                @pl.when(jnp.logical_not(here))
+                def _():
                     copy.start()
 
-                @pl.when(local)
+                @pl.when(here)
                 def _():
-                    frecv[m, parity, z // 2, y // 2] = fmsg[m]
-
-    sibling_copy = {}
+                    pltpu.make_async_copy(fmsg.at[m], slot, rsem.at[FACTOR + m]).start()
 
     def sibling_task(m):
-        for i in range(4):
-            for j in range(2):
-                got = arrival(factor_base[m] + 2 * i + j, frecv.at[m, core, i, j])
-                mine = (2 * j + core == y) & (2 * i + y // 2 == z) & (parity == core)
-
-                @pl.when(jnp.logical_not(mine))
-                def _(got=got):
-                    got.wait_recv()
-        sibling_copy[m] = send(frecv.at[m, core], frecv.at[m, core], sibling)
+        arrived(FACTOR + m, frecv.at[m, core])
+        remote(frecv.at[m, core], frecv.at[m, core], SIBLING_OUT + m, SIBLING + m, sibling).start()
 
     def fac_task(m):
-        arrival(sibling_copy[m], frecv.at[m, 1 - core]).wait_recv()
+        arrived(SIBLING + m, frecv.at[m, 1 - core])
         for p in range(2):
             for i in range(4):
                 for j in range(2):
-                    value, diagonal = decode(frecv.at[m, p, i, j])
+                    value, diagonal = decode(frecv.at[m, p, pl.ds((2 * i + j) * ROWS, ROWS)])
                     if m != 1:
                         value = value + jnp.where(eye, diagonal, 0.0)
                     hi, lo = split(value)
@@ -198,15 +164,12 @@
     def block_of(i):
         return pl.ds(pl.multiple_of((i % 4) * 128, 128), 128)
 
-    gathers = {}
-    scatters = {}
-
     def put(n, q, v):
         vown[n, q] = v
         encode(vsend.at[n, q], v)
-        gathers[n, q] = [
-            send(vsend.at[n, q], vrecv.at[n, q, d - 1], at(((x + 4 - d) % 4) * 4 + y, col))
-            for d in (2, 1, 3)]
+        for d in (2, 1, 3):
+            remote(vsend.at[n, q], vrecv.at[n, q, d - 1], GATHER_OUT, GATHER + n * Q + q,
+                   at(((x + 4 - d) % 4) * 4 + y, col)).start()
 
     def kernel_columns(panel, p):
         inner = lax.dot_general(
@@ -231,8 +194,7 @@
         hi, lo = split(vown[n, q])
         gbuf[block_of(x), 0:CH] = hi
         gbuf[block_of(x), CH:PAIR] = lo
-        for k, d in zip(gathers[n, q], (2, 1, 3)):
-            arrival(k, vrecv.at[n, q, d - 1]).wait_recv()
+        arrived(GATHER + n * Q + q, vrecv.at[n, q])
         for d in (1, 2, 3):
             value, _ = decode(vrecv.at[n, q, d - 1])
             hi, lo = split(value)
@@ -245,16 +207,14 @@
             both = jnp.dot(fbuf[n, 0, rows, :], v, preferred_element_type=F32)
             low = jnp.dot(fbuf[n, 1, rows, :], v_hi, preferred_element_type=F32)
             ptmp[rows, :] = both[:, 0:CH] + (both[:, CH:PAIR] + low)
-        ks = []
         for d in (2, 1, 3):
             encode(psend.at[n, q, d - 1], ptmp[block_of(y + 4 - d), :])
-            ks.append(send(psend.at[n, q, d - 1], precv.at[n, q, d - 1], at(x * 4 + (y + 4 - d) % 4, col)))
-        scatters[n, q] = ks
+            remote(psend.at[n, q, d - 1], precv.at[n, q, d - 1], SCATTER_OUT, SCATTER + n * Q + q,
+                   at(x * 4 + (y + 4 - d) % 4, col)).start()
         pown[n, q] = ptmp[block_of(y), :]
 
     def e_task(n, q):
-        for k, d in zip(scatters[n, q], (2, 1, 3)):
-            arrival(k, precv.at[n, q, d - 1]).wait_recv()
+        arrived(SCATTER + n * Q + q, precv.at[n, q])
         value = pown[n, q]
         for d in (1, 2, 3):
             value = value + decode(precv.at[n, q, d - 1])[0]
@@ -290,21 +250,34 @@
             e_task(n, q)
 
     ebuf[pl.ds(row, 1)] = esum[...][None]
-    spread = [send(esum, ebuf.at[row], at((row + d) % 16, col)) for d in range(1, 16)]
     for d in range(1, 16):
-        arrival(spread[d - 1], ebuf.at[(row + 16 - d) % 16]).wait_recv()
+        remote(esum, ebuf.at[row], SPREAD_OUT, SPREAD, at((row + d) % 16, col)).start()
+    arrived(SPREAD, ebuf.at[pl.ds(0, 15)])
     total = ebuf[0]
     for i in range(1, 16):
         total = total + ebuf[i]
     ex_out[...] = total * (1.0 / (2.0 * B))
 
-    for copy in sent:
-        copy.wait_send()
-    for copy, local in factor_sends.values():
-        @pl.when(jnp.logical_not(local))
-        def _(copy=copy):
-            copy.wait_send()
-    assert counter[0] <= N_SEND
+    departed(GATHER_OUT, vrecv)
+    departed(SCATTER_OUT, precv)
+    departed(SPREAD_OUT, ebuf.at[pl.ds(0, 15)])
+    for m in range(3):
+        departed(SIBLING_OUT + m, frecv.at[m, core])
+
+        @pl.when(here)
+        def _():
+            departed(FACTOR_OUT + m, frecv.at[m, 0, pl.ds(0, 7 * ROWS)])
+
+        @pl.when(jnp.logical_not(here))
+        def _():
+            departed(FACTOR_OUT + m, frecv.at[m, 0])
+
+
+def finish(first, second, explained, first_out, second_out, explained_out):
+    first_out[...] = first[...]
+    second_out[...] = second[...]
+    for q in range(Q):
+        explained_out[q * CH:(q + 1) * CH] = explained[q, :]
 
 
 def shards(inducing_desc, candidate_desc, first_inverse, coupling, second_inverse):
@@ -324,7 +297,7 @@
             pltpu.VMEM((W, Q * CH), BF16),
             pltpu.VMEM((3, 128, 128), F32),
             pltpu.VMEM((3, ROWS, 128), BF16),
-            pltpu.VMEM((3, 2, 4, 2, ROWS, 128), BF16),
+            pltpu.VMEM((3, 2, 8 * ROWS, 128), BF16),
             pltpu.VMEM((3, 2, 512, 512), BF16),
             pltpu.VMEM((3, Q, 128, CH), F32),
             pltpu.VMEM((3, Q, ROWS, CH), BF16),
@@ -339,12 +312,21 @@
             pltpu.VMEM((16, 8, 128), F32),
             pltpu.SemaphoreType.DMA((4 + Q // 2,)),
             pltpu.SemaphoreType.DMA((N_SEND,)),
-            pltpu.SemaphoreType.DMA((N_SEND,)),
+            pltpu.SemaphoreType.DMA((N_RECV,)),
         ],
         compiler_params=pltpu.CompilerParams(
             collective_id=0, has_side_effects=True, vmem_limit_bytes=60 * 1024 * 1024),
     )(inducing_desc, candidate_desc, first_inverse, coupling, second_inverse)
-    return first, second, explained[:Q].reshape(Q * CH)
+    return pl.pallas_call(
+        finish,
+        out_shape=(
+            jax.ShapeDtypeStruct((128, Q * CH), F32),
+            jax.ShapeDtypeStruct((128, Q * CH), F32),
+            jax.ShapeDtypeStruct((Q * CH,), F32),
+        ),
+        in_specs=[vmem] * 3,
+        out_specs=(vmem, vmem, vmem),
+    )(first, second, explained)
 
 
 def solution(mesh):

time: 75.1 us -> 67.4 us (0.90)
  local copies, waits for them, and re-layouts: 4.8 us -> 0 us
  Pallas kernels: 68.8 us -> 66.1 us
    pallas_call x1, Pallas kernels: 68.8 us -> 64.1 us  [shards(): pl.pallas_call(kernel, out_shape=(jax.ShapeDtypeStruct((128, Q * CH), F32...]
    unnamed x2 -> x0, local copies, waits for them, and re-layouts: 3.53 us -> none
    pallas_call x0 -> x1, Pallas kernels: none -> 2.02 us  [shards(): pl.pallas_call(finish, out_shape=(jax.ShapeDtypeStruct((128, Q * CH), F32...]
    reshape x1 -> x0, local copies, waits for them, and re-layouts: 1.27 us -> none  [shards(): return (first, second, explained[:Q].reshape(Q * CH))]
where the time goes in v3:
time: 67.4 us; the launch traced here: 66.7 us
  Pallas kernels  66.1 us (98%)
    pallas_call x1, Pallas kernels, shards(): pl.pallas_call(kernel, out_shape=(jax.ShapeDtypeStruct((128, Q * CH), F32...  64.1 us
    pallas_call x1, Pallas kernels, shards(): pl.pallas_call(finish, out_shape=(jax.ShapeDtypeStruct((128, Q * CH), F32...  2.02 us

profile of v3, /device:TPU:32, one launch (start us, length us, event | category | flops | bytes accessed | tf_op | source)
XLA Modules:
  0.0 66.7 jit_solution(11406277628953893938)
XLA Ops:
  0.6 64.1 %shard_map.76 = (f32[128,768]{1,0:T(8,128)}, f32[128,768]{1,0:T(8,128)}, f32[8,128]{1,0:T(8,128)}) custom-call(bf16[2,1960,128]{2,1,0:T(8,128)(2,1)} %desc_hbm.1, bf16[1960,768]{1,0:T(8,128)(2,1)} %cand_hbm.1, f32[128,128]{1,0:T(8,128)} %f_hbm.1, f32[128,128]{1,0:T(8,128)} %c_hbm.1, f32[128,128]{1,0:T(8,128)} %s_hbm.1), custom_call_target="tpu_custom_call" | custom-call | tf_op jit(solution)/shard_map/pallas_call | solution.py:286
  64.7 2.0 %shard_map.77 = (f32[128,768]{1,0:T(8,128)}, f32[128,768]{1,0:T(8,128)}, f32[768]{0:T(1024)}) custom-call(f32[128,768]{1,0:T(8,128)} %get-tuple-element.6.first, f32[128,768]{1,0:T(8,128)} %get-tuple-element.7.second, f32[8,128]{1,0:T(8,128)} %get-tuple-element.8.explained), custom_call_target="tpu_custom_call" | custom-call | tf_op jit(solution)/shard_map/pallas_call | solution.py:320

commit v4 on v3

--- a/solution.py
+++ b/solution.py
@@ -14,8 +14,8 @@
 F32 = jnp.float32
 BF16 = jnp.bfloat16
 
-GATHER, SCATTER, FACTOR, SIBLING, SPREAD, N_RECV = 0, 18, 36, 39, 42, 43
-GATHER_OUT, SCATTER_OUT, FACTOR_OUT, SIBLING_OUT, SPREAD_OUT, N_SEND = 0, 1, 2, 5, 8, 9
+GATHER, SCATTER, FACTOR, SIBLING, SPREAD, GATHER_C, SCATTER_T, N_RECV = 0, 18, 30, 33, 36, 37, 38, 39
+GATHER_OUT, SCATTER_OUT, FACTOR_OUT, SIBLING_OUT, SPREAD_OUT, C_OUT, T_OUT, N_SEND = 0, 1, 2, 5, 8, 9, 10, 11
 ROWS = 144
 TINY = 1e-35
 
@@ -50,28 +50,19 @@
     return jnp.where(c < 0.0, -t, t), tail[1:2, :] + tail[2:3, :]
 
 
-def task_order():
-    tasks = []
-    start, period, step, flight = 14.0, 10.6, 1.65, 5.2
-    for n in range(3):
-        for q in range(Q):
-            t = start + n * period + q * step
-            tasks.append((t, "c", n, q))
-            tasks.append((t + flight, "e", n, q))
-    for p in range(Q // 2):
-        tasks.append((3.0 + 0.5 * p, "k1", 0, p))
-        tasks.append((5.0 + 0.5 * p, "k2", 0, p))
-    for m in range(3):
-        tasks.append(((2.0, 7.0, 13.0)[m], "fsend", m, 0))
-        tasks.append(((10.0, 16.0, 24.0)[m], "sibling", m, 0))
-        tasks.append(((13.9, 20.0, 30.0)[m], "fac", m, 0))
-    tasks.sort()
-    return tasks
+TASKS = (
+    ("fsend", 2, 0), ("fsend", 0, 0), ("coupling", 0, 0), ("k", 0, 0), ("k", 0, 1), ("k", 0, 2), ("k", 1, 0),
+    ("k", 1, 1), ("k", 1, 2), ("sibling", 2, 0), ("fac", 2, 0), ("ct", 0, 0), ("sibling", 0, 0), ("et", 0, 0),
+    ("fac", 0, 0), ("c", 0, 0), ("c", 0, 1), ("c", 0, 2), ("c", 0, 3), ("c", 0, 4), ("c", 0, 5), ("e", 0, 0),
+    ("e", 0, 1), ("e", 0, 2), ("sibling", 1, 0), ("e", 0, 3), ("fac", 1, 0), ("c", 1, 0), ("e", 0, 4),
+    ("c", 1, 1), ("e", 0, 5), ("c", 1, 2), ("c", 1, 3), ("e", 1, 0), ("c", 1, 4), ("e", 1, 1), ("c", 1, 5),
+    ("e", 1, 2), ("e", 1, 3), ("e", 1, 4), ("e", 1, 5),
+)
 
 
 def kernel(desc_hbm, cand_hbm, f_hbm, c_hbm, s_hbm, first_out, second_out, ex_out,
            desc, cand, fin, fmsg, frecv, fbuf, vown, vsend, vrecv, gbuf, pown, ptmp, psend, precv,
-           k2, esum, ebuf, lsem, ssem, rsem):
+           csend, crecv, tsend, trecv, town, esum, ebuf, lsem, ssem, rsem):
     row = lax.axis_index("row")
     col = lax.axis_index("col")
     x, y = row // 4, row % 4
@@ -94,6 +85,14 @@
 
     def departed(out, ref):
         remote(ref, ref, out, 0, sibling).wait_send()
+
+    barrier = pltpu.get_barrier_semaphore()
+    partners = [at((row + d) % 16, col) for d in range(1, 16)] + [sibling]
+    for i in range(4):
+        for j in range(2):
+            partners.append(at(x * 4 + 2 * j + core, (2 * i + y // 2) * 2 + parity))
+    for device in partners:
+        pl.semaphore_signal(barrier, inc=1, device_id=device, device_id_type=MESH)
 
     loads = []
     for m, ref in enumerate((f_hbm, c_hbm, s_hbm)):
@@ -105,25 +104,14 @@
     for copy in loads:
         copy.start()
 
-    barrier = pltpu.get_barrier_semaphore()
-    partners = [at((row + d) % 16, col) for d in range(1, 16)] + [sibling]
-    for i in range(4):
-        for j in range(2):
-            partners.append(at(x * 4 + 2 * j + core, (2 * i + y // 2) * 2 + parity))
-    for device in partners:
-        pl.semaphore_signal(barrier, inc=1, device_id=device, device_id_type=MESH)
-
     eye = lax.broadcasted_iota(jnp.int32, (128, 128), 0) == lax.broadcasted_iota(jnp.int32, (128, 128), 1)
     on_diagonal = row == col
     def encode_factor(m):
         loads[m].wait()
         block = fin[m]
-        if m == 1:
-            encode(fmsg.at[m], block, jnp.zeros((1, 128), F32))
-        else:
-            taken = eye & on_diagonal
-            diagonal = jnp.sum(jnp.where(taken, block, 0.0), axis=0, keepdims=True)
-            encode(fmsg.at[m], jnp.where(taken, 0.0, block), diagonal)
+        taken = eye & on_diagonal
+        diagonal = jnp.sum(jnp.where(taken, block, 0.0), axis=0, keepdims=True)
+        encode(fmsg.at[m], jnp.where(taken, 0.0, block), diagonal)
 
     here = (to_y == y) & (core == parity)
     my_slot = pl.ds(pl.multiple_of(((z // 2) * 2 + y // 2) * ROWS, 16), ROWS)
@@ -164,12 +152,26 @@
     def block_of(i):
         return pl.ds(pl.multiple_of((i % 4) * 128, 128), 128)
 
+    def spread_over(send_ref, recv_ref, out, into, d, device):
+        remote(send_ref, recv_ref.at[d - 1], out, into, device).start()
+
+    def over_x(d):
+        return at(((x + 4 - d) % 4) * 4 + y, col)
+
+    def over_y(d):
+        return at(x * 4 + (y + 4 - d) % 4, col)
+
     def put(n, q, v):
         vown[n, q] = v
         encode(vsend.at[n, q], v)
         for d in (2, 1, 3):
-            remote(vsend.at[n, q], vrecv.at[n, q, d - 1], GATHER_OUT, GATHER + n * Q + q,
-                   at(((x + 4 - d) % 4) * 4 + y, col)).start()
+            spread_over(vsend.at[n, q], vrecv.at[n, q], GATHER_OUT, GATHER + n * Q + q, d, over_x(d))
+
+    def coupling_task():
+        loads[1].wait()
+        encode(csend, fin[1])
+        for d in (2, 1, 3):
+            spread_over(csend, crecv, C_OUT, GATHER_C, d, over_x(d))
 
     def kernel_columns(panel, p):
         inner = lax.dot_general(
@@ -177,77 +179,93 @@
             preferred_element_type=F32)
         return inner * inner
 
-    def k1_task(p):
-        if p == 0:
-            loads[3].wait()
-        loads[4 + p].wait()
-        value = kernel_columns(0, p)
+    def k_task(panel, p):
+        if panel == 0:
+            if p == 0:
+                loads[3].wait()
+            loads[4 + p].wait()
+        value = kernel_columns(panel, p)
         for i in range(2):
-            put(0, 2 * p + i, value[:, i * CH:(i + 1) * CH])
-
-    def k2_task(p):
-        value = kernel_columns(1, p)
-        for i in range(2):
-            k2[2 * p + i] = value[:, i * CH:(i + 1) * CH]
+            put(panel, 2 * p + i, value[:, i * CH:(i + 1) * CH])
+
+    def fill(g, own, recv):
+        hi, lo = split(own)
+        gbuf[g, block_of(x), 0:CH] = hi
+        gbuf[g, block_of(x), CH:PAIR] = lo
+        for d in (1, 2, 3):
+            hi, lo = split(decode(recv.at[d - 1])[0])
+            gbuf[g, block_of(x + d), 0:CH] = hi
+            gbuf[g, block_of(x + d), CH:PAIR] = lo
+
+    def product(m, g, rows):
+        both = jnp.dot(fbuf[m, 0, rows, :], gbuf[g], preferred_element_type=F32)
+        low = jnp.dot(fbuf[m, 1, rows, :], gbuf[g, :, 0:CH], preferred_element_type=F32)
+        return both[:, 0:CH] + (both[:, CH:PAIR] + low)
+
+    def scatter(send_ref, recv_ref, out, into):
+        for d in (2, 1, 3):
+            encode(send_ref.at[d - 1], ptmp[block_of(y + 4 - d), :])
+            spread_over(send_ref.at[d - 1], recv_ref, out, into, d, over_y(d))
+
+    def collect(own, recv):
+        value = own
+        for d in (1, 2, 3):
+            value = value + decode(recv.at[d - 1])[0]
+        return value
+
+    halves = (slice(0, 256), slice(256, 512))
+
+    def ct_task():
+        arrived(GATHER_C, crecv)
+        fill(0, fin[1], crecv)
+        for rows in halves:
+            ptmp[rows, :] = product(2, 0, rows)
+        scatter(tsend, trecv, T_OUT, SCATTER_T)
+        town[...] = ptmp[block_of(y), :]
+
+    def et_task():
+        arrived(SCATTER_T, trecv)
+        encode(fmsg.at[1], collect(town[...], trecv), jnp.zeros((1, 128), F32))
+        fsend_task(1)
 
     def c_task(n, q):
-        hi, lo = split(vown[n, q])
-        gbuf[block_of(x), 0:CH] = hi
-        gbuf[block_of(x), CH:PAIR] = lo
         arrived(GATHER + n * Q + q, vrecv.at[n, q])
-        for d in (1, 2, 3):
-            value, _ = decode(vrecv.at[n, q, d - 1])
-            hi, lo = split(value)
-            gbuf[block_of(x + d), 0:CH] = hi
-            gbuf[block_of(x + d), CH:PAIR] = lo
-        v = gbuf[...]
-        v_hi = v[:, 0:CH]
-        for i in range(2):
-            rows = slice(i * 256, (i + 1) * 256)
-            both = jnp.dot(fbuf[n, 0, rows, :], v, preferred_element_type=F32)
-            low = jnp.dot(fbuf[n, 1, rows, :], v_hi, preferred_element_type=F32)
-            ptmp[rows, :] = both[:, 0:CH] + (both[:, CH:PAIR] + low)
-        for d in (2, 1, 3):
-            encode(psend.at[n, q, d - 1], ptmp[block_of(y + 4 - d), :])
-            remote(psend.at[n, q, d - 1], precv.at[n, q, d - 1], SCATTER_OUT, SCATTER + n * Q + q,
-                   at(x * 4 + (y + 4 - d) % 4, col)).start()
+        fill(0, vown[n, q], vrecv.at[n, q])
+        if n == 0:
+            for rows in halves:
+                ptmp[rows, :] = product(0, 0, rows)
+        else:
+            arrived(GATHER + 2 * Q + q, vrecv.at[2, q])
+            fill(1, vown[2, q], vrecv.at[2, q])
+            for rows in halves:
+                ptmp[rows, :] = product(2, 0, rows) - product(1, 1, rows)
+        scatter(psend.at[n, q], precv.at[n, q], SCATTER_OUT, SCATTER + n * Q + q)
         pown[n, q] = ptmp[block_of(y), :]
 
     def e_task(n, q):
         arrived(SCATTER + n * Q + q, precv.at[n, q])
-        value = pown[n, q]
-        for d in (1, 2, 3):
-            value = value + decode(precv.at[n, q, d - 1])[0]
+        value = collect(pown[n, q], precv.at[n, q])
         columns = slice(q * CH, (q + 1) * CH)
         if n == 0:
-            put(1, q, value)
+            put(2, q, value)
             first_out[:, columns] = value
             esum[q:q + 1, :] = jnp.sum(value * value, axis=0, keepdims=True)
-        elif n == 1:
-            put(2, q, k2[q] - value)
         else:
             esum[q:q + 1, :] = esum[q:q + 1, :] + jnp.sum(value * value, axis=0, keepdims=True)
             second_out[:, columns] = value
 
     esum[...] = jnp.zeros_like(esum)
-    for m in range(3):
-        encode_factor(m)
+    encode_factor(2)
+    encode_factor(0)
     pl.semaphore_wait(barrier, len(partners))
-    for _, name, n, q in task_order():
-        if name == "fsend":
-            fsend_task(n)
-        elif name == "sibling":
-            sibling_task(n)
-        elif name == "fac":
-            fac_task(n)
-        elif name == "k1":
-            k1_task(q)
-        elif name == "k2":
-            k2_task(q)
-        elif name == "c":
-            c_task(n, q)
-        else:
-            e_task(n, q)
+    run = {
+        "fsend": lambda n, q: fsend_task(n), "sibling": lambda n, q: sibling_task(n),
+        "fac": lambda n, q: fac_task(n), "coupling": lambda n, q: coupling_task(),
+        "k": k_task, "ct": lambda n, q: ct_task(), "et": lambda n, q: et_task(),
+        "c": c_task, "e": e_task,
+    }
+    for name, n, q in TASKS:
+        run[name](n, q)
 
     ebuf[pl.ds(row, 1)] = esum[...][None]
     for d in range(1, 16):
@@ -260,6 +278,8 @@
 
     departed(GATHER_OUT, vrecv)
     departed(SCATTER_OUT, precv)
+    departed(C_OUT, crecv)
+    departed(T_OUT, trecv)
     departed(SPREAD_OUT, ebuf.at[pl.ds(0, 15)])
     for m in range(3):
         departed(SIBLING_OUT + m, frecv.at[m, core])
@@ -302,12 +322,16 @@
             pltpu.VMEM((3, Q, 128, CH), F32),
             pltpu.VMEM((3, Q, ROWS, CH), BF16),
             pltpu.VMEM((3, Q, 3, ROWS, CH), BF16),
-            pltpu.VMEM((512, PAIR), BF16),
-            pltpu.VMEM((3, Q, 128, CH), F32),
+            pltpu.VMEM((2, 512, PAIR), BF16),
+            pltpu.VMEM((2, Q, 128, CH), F32),
             pltpu.VMEM((512, CH), F32),
-            pltpu.VMEM((3, Q, 3, ROWS, CH), BF16),
-            pltpu.VMEM((3, Q, 3, ROWS, CH), BF16),
-            pltpu.VMEM((Q, 128, CH), F32),
+            pltpu.VMEM((2, Q, 3, ROWS, CH), BF16),
+            pltpu.VMEM((2, Q, 3, ROWS, CH), BF16),
+            pltpu.VMEM((ROWS, 128), BF16),
+            pltpu.VMEM((3, ROWS, 128), BF16),
+            pltpu.VMEM((3, ROWS, 128), BF16),
+            pltpu.VMEM((3, ROWS, 128), BF16),
+            pltpu.VMEM((128, 128), F32),
             pltpu.VMEM((8, 128), F32),
             pltpu.VMEM((16, 8, 128), F32),
             pltpu.SemaphoreType.DMA((4 + Q // 2,)),

time: 67.4 us -> 64.4 us (0.955)
  Pallas kernels: 66.1 us -> 63.1 us
    pallas_call x1, Pallas kernels: 64.1 us -> 61.1 us  [shards(): pl.pallas_call(kernel, out_shape=(jax.ShapeDtypeStruct((128, Q * CH), F32...]
where the time goes in v4:
time: 64.4 us; the launch traced here: 63.8 us
  Pallas kernels  63.1 us (98%)
    pallas_call x1, Pallas kernels, shards(): pl.pallas_call(kernel, out_shape=(jax.ShapeDtypeStruct((128, Q * CH), F32...  61.1 us
    pallas_call x1, Pallas kernels, shards(): pl.pallas_call(finish, out_shape=(jax.ShapeDtypeStruct((128, Q * CH), F32...  2.02 us

profile of v4, /device:TPU:32, one launch (start us, length us, event | category | flops | bytes accessed | tf_op | source)
XLA Modules:
  0.0 63.8 jit_solution(17312753161579930123)
XLA Ops:
  0.6 61.1 %shard_map.76 = (f32[128,768]{1,0:T(8,128)}, f32[128,768]{1,0:T(8,128)}, f32[8,128]{1,0:T(8,128)}) custom-call(bf16[2,1960,128]{2,1,0:T(8,128)(2,1)} %desc_hbm.1, bf16[1960,768]{1,0:T(8,128)(2,1)} %cand_hbm.1, f32[128,128]{1,0:T(8,128)} %f_hbm.1, f32[128,128]{1,0:T(8,128)} %c_hbm.1, f32[128,128]{1,0:T(8,128)} %s_hbm.1), custom_call_target="tpu_custom_call" | custom-call | tf_op jit(solution)/shard_map/pallas_call | solution.py:306
  61.8 2.0 %shard_map.77 = (f32[128,768]{1,0:T(8,128)}, f32[128,768]{1,0:T(8,128)}, f32[768]{0:T(1024)}) custom-call(f32[128,768]{1,0:T(8,128)} %get-tuple-element.6.first, f32[128,768]{1,0:T(8,128)} %get-tuple-element.7.second, f32[8,128]{1,0:T(8,128)} %get-tuple-element.8.explained), custom_call_target="tpu_custom_call" | custom-call | tf_op jit(solution)/shard_map/pallas_call | solution.py:344

commit v5 on v4

--- a/solution.py
+++ b/solution.py
@@ -14,7 +14,7 @@
 F32 = jnp.float32
 BF16 = jnp.bfloat16
 
-GATHER, SCATTER, FACTOR, SIBLING, SPREAD, GATHER_C, SCATTER_T, N_RECV = 0, 18, 30, 33, 36, 37, 38, 39
+GATHER, SCATTER, FACTOR, SIBLING, SPREAD, GATHER_C, SCATTER_T, N_RECV = 0, 18, 30, 42, 45, 46, 47, 48
 GATHER_OUT, SCATTER_OUT, FACTOR_OUT, SIBLING_OUT, SPREAD_OUT, C_OUT, T_OUT, N_SEND = 0, 1, 2, 5, 8, 9, 10, 11
 ROWS = 144
 TINY = 1e-35
@@ -53,16 +53,17 @@
 TASKS = (
     ("fsend", 2, 0), ("fsend", 0, 0), ("coupling", 0, 0), ("k", 0, 0), ("k", 0, 1), ("k", 0, 2), ("k", 1, 0),
     ("k", 1, 1), ("k", 1, 2), ("sibling", 2, 0), ("fac", 2, 0), ("ct", 0, 0), ("sibling", 0, 0), ("et", 0, 0),
-    ("fac", 0, 0), ("c", 0, 0), ("c", 0, 1), ("c", 0, 2), ("c", 0, 3), ("c", 0, 4), ("c", 0, 5), ("e", 0, 0),
-    ("e", 0, 1), ("e", 0, 2), ("sibling", 1, 0), ("e", 0, 3), ("fac", 1, 0), ("c", 1, 0), ("e", 0, 4),
-    ("c", 1, 1), ("e", 0, 5), ("c", 1, 2), ("c", 1, 3), ("e", 1, 0), ("c", 1, 4), ("e", 1, 1), ("c", 1, 5),
-    ("e", 1, 2), ("e", 1, 3), ("e", 1, 4), ("e", 1, 5),
+    ("fac", 0, 0), ("c", 0, 0), ("c", 0, 1), ("c", 0, 2), ("c", 0, 3), ("c", 0, 4), ("c", 0, 5), ("s", 0, 0),
+    ("s", 0, 1), ("s", 0, 2), ("s", 0, 3), ("e", 0, 0), ("s", 0, 4), ("e", 0, 1), ("s", 0, 5), ("e", 0, 2),
+    ("sibling", 1, 0), ("e", 0, 3), ("fac", 1, 0), ("c", 1, 0), ("e", 0, 4), ("c", 1, 1), ("e", 0, 5),
+    ("c", 1, 2), ("c", 1, 3), ("e", 1, 0), ("c", 1, 4), ("e", 1, 1), ("c", 1, 5), ("e", 1, 2), ("e", 1, 3),
+    ("e", 1, 4), ("e", 1, 5),
 )
 
 
 def kernel(desc_hbm, cand_hbm, f_hbm, c_hbm, s_hbm, first_out, second_out, ex_out,
            desc, cand, fin, fmsg, frecv, fbuf, vown, vsend, vrecv, gbuf, pown, ptmp, psend, precv,
-           csend, crecv, tsend, trecv, town, esum, ebuf, lsem, ssem, rsem):
+           csend, crecv, tsend, trecv, town, sk2, second, esum, ebuf, lsem, ssem, rsem):
     row = lax.axis_index("row")
     col = lax.axis_index("col")
     x, y = row // 4, row % 4
@@ -87,10 +88,11 @@
         remote(ref, ref, out, 0, sibling).wait_send()
 
     barrier = pltpu.get_barrier_semaphore()
-    partners = [at((row + d) % 16, col) for d in range(1, 16)] + [sibling]
+    partners = []
     for i in range(4):
         for j in range(2):
-            partners.append(at(x * 4 + 2 * j + core, (2 * i + y // 2) * 2 + parity))
+            partners.append(at(x * 4 + 2 * j + core, (2 * ((z // 2 + i + 1) % 4) + y // 2) * 2 + parity))
+    partners += [at((row + d) % 16, col) for d in range(1, 16)] + [sibling]
     for device in partners:
         pl.semaphore_signal(barrier, inc=1, device_id=device, device_id_type=MESH)
 
@@ -119,8 +121,9 @@
     def fsend_task(m):
         slot = frecv.at[m, parity, my_slot]
         for dz in (4, 3, 5, 2, 6, 1, 7, 0):
-            copy = remote(fmsg.at[m], slot, FACTOR_OUT + m, FACTOR + m,
-                          at(x * 4 + to_y, ((z + dz) % 8) * 2 + parity))
+            to_z = (z + dz) % 8
+            into = FACTOR + 4 * m + (z // 2 + 4 - to_z // 2) % 4
+            copy = remote(fmsg.at[m], slot, FACTOR_OUT + m, into, at(x * 4 + to_y, to_z * 2 + parity))
             if dz:
                 copy.start()
             else:
@@ -130,24 +133,30 @@
 
                 @pl.when(here)
                 def _():
-                    pltpu.make_async_copy(fmsg.at[m], slot, rsem.at[FACTOR + m]).start()
+                    pltpu.make_async_copy(fmsg.at[m], slot, rsem.at[FACTOR + 4 * m]).start()
 
     def sibling_task(m):
-        arrived(FACTOR + m, frecv.at[m, core])
-        remote(frecv.at[m, core], frecv.at[m, core], SIBLING_OUT + m, SIBLING + m, sibling).start()
+        for k in (2, 1, 3, 0):
+            strip = (z // 2 + k) % 4
+            got = frecv.at[m, core, pl.ds(pl.multiple_of(strip * (2 * ROWS), 2 * ROWS), 2 * ROWS)]
+            arrived(FACTOR + 4 * m + k, got)
+            remote(got, got, SIBLING_OUT + m, SIBLING + m, sibling).start()
+        decode_factor(m, core)
+
+    def decode_factor(m, p):
+        for i in range(4):
+            for j in range(2):
+                value, diagonal = decode(frecv.at[m, p, pl.ds((2 * i + j) * ROWS, ROWS)])
+                if m != 1:
+                    value = value + jnp.where(eye, diagonal, 0.0)
+                hi, lo = split(value)
+                rows = pl.ds(pl.multiple_of(2 * j * 128 + p * 128, 128), 128)
+                fbuf[m, 0, rows, i * 128:(i + 1) * 128] = hi
+                fbuf[m, 1, rows, i * 128:(i + 1) * 128] = lo
 
     def fac_task(m):
         arrived(SIBLING + m, frecv.at[m, 1 - core])
-        for p in range(2):
-            for i in range(4):
-                for j in range(2):
-                    value, diagonal = decode(frecv.at[m, p, pl.ds((2 * i + j) * ROWS, ROWS)])
-                    if m != 1:
-                        value = value + jnp.where(eye, diagonal, 0.0)
-                    hi, lo = split(value)
-                    r = (2 * j + p) * 128
-                    fbuf[m, 0, r:r + 128, i * 128:(i + 1) * 128] = hi
-                    fbuf[m, 1, r:r + 128, i * 128:(i + 1) * 128] = lo
+        decode_factor(m, 1 - core)
 
     def block_of(i):
         return pl.ds(pl.multiple_of((i % 4) * 128, 128), 128)
@@ -228,17 +237,19 @@
         encode(fmsg.at[1], collect(town[...], trecv), jnp.zeros((1, 128), F32))
         fsend_task(1)
 
+    def s_task(q):
+        arrived(GATHER + Q + q, vrecv.at[1, q])
+        fill(0, vown[1, q], vrecv.at[1, q])
+        for rows in halves:
+            sk2[q, rows, :] = product(2, 0, rows)
+
     def c_task(n, q):
-        arrived(GATHER + n * Q + q, vrecv.at[n, q])
-        fill(0, vown[n, q], vrecv.at[n, q])
-        if n == 0:
-            for rows in halves:
-                ptmp[rows, :] = product(0, 0, rows)
-        else:
-            arrived(GATHER + 2 * Q + q, vrecv.at[2, q])
-            fill(1, vown[2, q], vrecv.at[2, q])
-            for rows in halves:
-                ptmp[rows, :] = product(2, 0, rows) - product(1, 1, rows)
+        k = 2 * n
+        arrived(GATHER + k * Q + q, vrecv.at[k, q])
+        fill(0, vown[k, q], vrecv.at[k, q])
+        for rows in halves:
+            value = product(n, 0, rows)
+            ptmp[rows, :] = value if n == 0 else sk2[q, rows, :] - value
         scatter(psend.at[n, q], precv.at[n, q], SCATTER_OUT, SCATTER + n * Q + q)
         pown[n, q] = ptmp[block_of(y), :]
 
@@ -248,11 +259,12 @@
         columns = slice(q * CH, (q + 1) * CH)
         if n == 0:
             put(2, q, value)
-            first_out[:, columns] = value
+            pltpu.make_async_copy(vown.at[2, q], first_out.at[:, columns], lsem.at[4 + Q // 2]).start()
             esum[q:q + 1, :] = jnp.sum(value * value, axis=0, keepdims=True)
         else:
             esum[q:q + 1, :] = esum[q:q + 1, :] + jnp.sum(value * value, axis=0, keepdims=True)
-            second_out[:, columns] = value
+            second[q] = value
+            pltpu.make_async_copy(second.at[q], second_out.at[:, columns], lsem.at[5 + Q // 2]).start()
 
     esum[...] = jnp.zeros_like(esum)
     encode_factor(2)
@@ -261,7 +273,7 @@
     run = {
         "fsend": lambda n, q: fsend_task(n), "sibling": lambda n, q: sibling_task(n),
         "fac": lambda n, q: fac_task(n), "coupling": lambda n, q: coupling_task(),
-        "k": k_task, "ct": lambda n, q: ct_task(), "et": lambda n, q: et_task(),
+        "k": k_task, "s": lambda n, q: s_task(q), "ct": lambda n, q: ct_task(), "et": lambda n, q: et_task(),
         "c": c_task, "e": e_task,
     }
     for name, n, q in TASKS:
@@ -276,6 +288,8 @@
         total = total + ebuf[i]
     ex_out[...] = total * (1.0 / (2.0 * B))
 
+    pltpu.make_async_copy(first_out, first_out, lsem.at[4 + Q // 2]).wait()
+    pltpu.make_async_copy(second_out, second_out, lsem.at[5 + Q // 2]).wait()
     departed(GATHER_OUT, vrecv)
     departed(SCATTER_OUT, precv)
     departed(C_OUT, crecv)
@@ -311,7 +325,7 @@
             jax.ShapeDtypeStruct((8, 128), F32),
         ),
         in_specs=[hbm] * 5,
-        out_specs=(vmem, vmem, vmem),
+        out_specs=(hbm, hbm, vmem),
         scratch_shapes=[
             pltpu.VMEM((2, W, 128), BF16),
             pltpu.VMEM((W, Q * CH), BF16),
@@ -322,7 +336,7 @@
             pltpu.VMEM((3, Q, 128, CH), F32),
             pltpu.VMEM((3, Q, ROWS, CH), BF16),
             pltpu.VMEM((3, Q, 3, ROWS, CH), BF16),
-            pltpu.VMEM((2, 512, PAIR), BF16),
+            pltpu.VMEM((1, 512, PAIR), BF16),
             pltpu.VMEM((2, Q, 128, CH), F32),
             pltpu.VMEM((512, CH), F32),
             pltpu.VMEM((2, Q, 3, ROWS, CH), BF16),
@@ -332,9 +346,11 @@
             pltpu.VMEM((3, ROWS, 128), BF16),
             pltpu.VMEM((3, ROWS, 128), BF16),
             pltpu.VMEM((128, 128), F32),
+            pltpu.VMEM((Q, 512, CH), F32),
+            pltpu.VMEM((Q, 128, CH), F32),
             pltpu.VMEM((8, 128), F32),
             pltpu.VMEM((16, 8, 128), F32),
-            pltpu.SemaphoreType.DMA((4 + Q // 2,)),
+            pltpu.SemaphoreType.DMA((6 + Q // 2,)),
             pltpu.SemaphoreType.DMA((N_SEND,)),
             pltpu.SemaphoreType.DMA((N_RECV,)),
         ],

time: 64.4 us -> 62.7 us (0.974)
  Pallas kernels: 63.1 us -> 61.7 us
    pallas_call x1, Pallas kernels: 61.1 us -> 59.7 us  [shards(): pl.pallas_call(kernel, out_shape=(jax.ShapeDtypeStruct((128, Q * CH), F32...]
where the time goes in v5:
time: 62.7 us; the launch traced here: 62.3 us
  Pallas kernels  61.7 us (98%)
  between operations  0.64 us (1%)
    pallas_call x1, Pallas kernels, shards(): pl.pallas_call(kernel, out_shape=(jax.ShapeDtypeStruct((128, Q * CH), F32...  59.7 us
    pallas_call x1, Pallas kernels, shards(): pl.pallas_call(finish, out_shape=(jax.ShapeDtypeStruct((128, Q * CH), F32...  2.02 us

profile of v5, /device:TPU:32, one launch (start us, length us, event | category | flops | bytes accessed | tf_op | source)
XLA Modules:
  0.0 62.3 jit_solution(4106242590556808645)
XLA Ops:
  0.6 59.7 %shard_map.76 = (f32[128,768]{1,0:T(8,128)}, f32[128,768]{1,0:T(8,128)}, f32[8,128]{1,0:T(8,128)}) custom-call(bf16[2,1960,128]{2,1,0:T(8,128)(2,1)} %desc_hbm.1, bf16[1960,768]{1,0:T(8,128)(2,1)} %cand_hbm.1, f32[128,128]{1,0:T(8,128)} %f_hbm.1, f32[128,128]{1,0:T(8,128)} %c_hbm.1, f32[128,128]{1,0:T(8,128)} %s_hbm.1), custom_call_target="tpu_custom_call" | custom-call | tf_op jit(solution)/shard_map/pallas_call | solution.py:320
  60.3 2.0 %shard_map.77 = (f32[128,768]{1,0:T(8,128)}, f32[128,768]{1,0:T(8,128)}, f32[768]{0:T(1024)}) custom-call(f32[128,768]{1,0:T(8,128)} %get-tuple-element.6.first, f32[128,768]{1,0:T(8,128)} %get-tuple-element.7.second, f32[8,128]{1,0:T(8,128)} %get-tuple-element.8.explained), custom_call_target="tpu_custom_call" | custom-call | tf_op jit(solution)/shard_map/pallas_call | solution.py:360

commit v6 on v5

--- a/solution.py
+++ b/solution.py
@@ -15,7 +15,7 @@
 BF16 = jnp.bfloat16
 
 GATHER, SCATTER, FACTOR, SIBLING, SPREAD, GATHER_C, SCATTER_T, N_RECV = 0, 18, 30, 42, 45, 46, 47, 48
-GATHER_OUT, SCATTER_OUT, FACTOR_OUT, SIBLING_OUT, SPREAD_OUT, C_OUT, T_OUT, N_SEND = 0, 1, 2, 5, 8, 9, 10, 11
+GATHER_OUT, SCATTER_OUT, FACTOR_OUT, SIBLING_OUT, SPREAD_OUT, C_OUT, T_OUT, LAST_OUT, N_SEND = 0, 1, 2, 5, 8, 9, 10, 11, 12
 ROWS = 144
 TINY = 1e-35
 
@@ -26,14 +26,26 @@
     return hi, lo
 
 
+def codes_of(v, s):
+    t = jnp.abs(v) * (250.0 / s)
+    e = jnp.floor(t)
+    c = jnp.exp2(e - 125.0) * ((t - e) + 1.0)
+    return jnp.where(v < 0.0, -c, c).astype(BF16)
+
+
+def values_of(c, s):
+    c = c.astype(F32)
+    a = jnp.abs(c)
+    e = jnp.floor(jnp.log2(a) + 0.002)
+    t = (e + (a * jnp.exp2(-e) + 124.0)) * (s * (1.0 / 250.0))
+    return jnp.where(c < 0.0, -t, t)
+
+
 def encode(ref, v, diagonal=None):
     top = jnp.max(jnp.abs(v), axis=0, keepdims=True)
-    s = (top * 1.01 + TINY).astype(BF16)
-    t = jnp.abs(v) * (250.0 / s.astype(F32))
-    e = jnp.floor(t)
-    c = jnp.exp2(e - 125.0) * ((t - e) + 1.0)
-    ref[0:128, :] = jnp.where(v < 0.0, -c, c).astype(BF16)
-    tail = jnp.broadcast_to(s.astype(F32), (16, 128))
+    s = (top * 1.01 + TINY).astype(BF16).astype(F32)
+    ref[0:128, :] = codes_of(v, s)
+    tail = jnp.broadcast_to(s, (16, 128))
     if diagonal is not None:
         hi, lo = split(diagonal)
         index = lax.broadcasted_iota(jnp.int32, (16, 128), 0)
@@ -42,12 +54,8 @@
 
 
 def decode(ref):
-    c = ref[0:128, :].astype(F32)
     tail = ref[128:144, :].astype(F32)
-    a = jnp.abs(c)
-    e = jnp.floor(jnp.log2(a) + 0.002)
-    t = (e + (a * jnp.exp2(-e) + 124.0)) * (tail[0:1, :] * (1.0 / 250.0))
-    return jnp.where(c < 0.0, -t, t), tail[1:2, :] + tail[2:3, :]
+    return values_of(ref[0:128, :], tail[0:1, :]), tail[1:2, :] + tail[2:3, :]
 
 
 TASKS = (
@@ -216,6 +224,33 @@
             encode(send_ref.at[d - 1], ptmp[block_of(y + 4 - d), :])
             spread_over(send_ref.at[d - 1], recv_ref, out, into, d, over_y(d))
 
+    scales = {}
+
+    def scatter_last(q):
+        place = q % 3
+        rows = ROWS if place == 2 else 128
+        for d in (2, 1, 3):
+            ref = psend.at[1, q, d - 1]
+            v = ptmp[block_of(y + 4 - d), :]
+            top = jnp.max(jnp.abs(v), axis=0, keepdims=True)
+            scale = (top * 1.01 + TINY).astype(BF16).astype(F32)
+            scales[place, d] = scale
+            ref[0:128, :] = codes_of(v, scale)
+            if place == 2:
+                index = lax.broadcasted_iota(jnp.int32, (16, 128), 0)
+                tail = jnp.where(index == 0, scales[0, d], jnp.where(index == 1, scales[1, d], scale))
+                ref[128:144, :] = tail.astype(BF16)
+            remote(psend.at[1, q, d - 1, pl.ds(0, rows)], precv.at[1, q, d - 1, pl.ds(0, rows)],
+                   LAST_OUT, SCATTER + Q + q, over_y(d)).start()
+
+    def collect_last(q):
+        value = pown[1, q]
+        last = q - q % 3 + 2
+        for d in (1, 2, 3):
+            tail = precv[1, last, d - 1, 128:144, :].astype(F32)
+            value = value + values_of(precv[1, q, d - 1, 0:128, :], tail[q % 3:q % 3 + 1, :])
+        return value
+
     def collect(own, recv):
         value = own
         for d in (1, 2, 3):
@@ -250,21 +285,30 @@
         for rows in halves:
             value = product(n, 0, rows)
             ptmp[rows, :] = value if n == 0 else sk2[q, rows, :] - value
-        scatter(psend.at[n, q], precv.at[n, q], SCATTER_OUT, SCATTER + n * Q + q)
+        if n == 0:
+            scatter(psend.at[n, q], precv.at[n, q], SCATTER_OUT, SCATTER + n * Q + q)
+        else:
+            scatter_last(q)
         pown[n, q] = ptmp[block_of(y), :]
 
     def e_task(n, q):
-        arrived(SCATTER + n * Q + q, precv.at[n, q])
-        value = collect(pown[n, q], precv.at[n, q])
-        columns = slice(q * CH, (q + 1) * CH)
         if n == 0:
+            arrived(SCATTER + q, precv.at[0, q])
+            value = collect(pown[0, q], precv.at[0, q])
             put(2, q, value)
+            columns = slice(q * CH, (q + 1) * CH)
             pltpu.make_async_copy(vown.at[2, q], first_out.at[:, columns], lsem.at[4 + Q // 2]).start()
             esum[q:q + 1, :] = jnp.sum(value * value, axis=0, keepdims=True)
-        else:
-            esum[q:q + 1, :] = esum[q:q + 1, :] + jnp.sum(value * value, axis=0, keepdims=True)
-            second[q] = value
-            pltpu.make_async_copy(second.at[q], second_out.at[:, columns], lsem.at[5 + Q // 2]).start()
+        elif q % 3 == 2:
+            for p in (q - 2, q - 1, q):
+                rows = ROWS if p == q else 128
+                arrived(SCATTER + Q + p, precv.at[1, p, :, pl.ds(0, rows)])
+            for p in (q - 2, q - 1, q):
+                value = collect_last(p)
+                columns = slice(p * CH, (p + 1) * CH)
+                second[p] = value
+                pltpu.make_async_copy(second.at[p], second_out.at[:, columns], lsem.at[5 + Q // 2]).start()
+                esum[p:p + 1, :] = esum[p:p + 1, :] + jnp.sum(value * value, axis=0, keepdims=True)
 
     esum[...] = jnp.zeros_like(esum)
     encode_factor(2)
@@ -291,7 +335,8 @@
     pltpu.make_async_copy(first_out, first_out, lsem.at[4 + Q // 2]).wait()
     pltpu.make_async_copy(second_out, second_out, lsem.at[5 + Q // 2]).wait()
     departed(GATHER_OUT, vrecv)
-    departed(SCATTER_OUT, precv)
+    departed(SCATTER_OUT, precv.at[0])
+    departed(LAST_OUT, sk2.at[:, pl.ds(0, 200)])
     departed(C_OUT, crecv)
     departed(T_OUT, trecv)
     departed(SPREAD_OUT, ebuf.at[pl.ds(0, 15)])

time: 62.7 us -> 62.2 us (level)
  no operation moved by 1% of the time
where the time goes in v6:
time: 62.2 us; the launch traced here: 61.9 us
  Pallas kernels  61.2 us (98%)
  between operations  0.64 us (1%)
    pallas_call x1, Pallas kernels, shards(): pl.pallas_call(kernel, out_shape=(jax.ShapeDtypeStruct((128, Q * CH), F32...  59.2 us
    pallas_call x1, Pallas kernels, shards(): pl.pallas_call(finish, out_shape=(jax.ShapeDtypeStruct((128, Q * CH), F32...  2.02 us

profile of v6, /device:TPU:32, one launch (start us, length us, event | category | flops | bytes accessed | tf_op | source)
XLA Modules:
  0.0 61.9 jit_solution(9557341929283143520)
XLA Ops:
  0.6 59.2 %shard_map.76 = (f32[128,768]{1,0:T(8,128)}, f32[128,768]{1,0:T(8,128)}, f32[8,128]{1,0:T(8,128)}) custom-call(bf16[2,1960,128]{2,1,0:T(8,128)(2,1)} %desc_hbm.1, bf16[1960,768]{1,0:T(8,128)(2,1)} %cand_hbm.1, f32[128,128]{1,0:T(8,128)} %f_hbm.1, f32[128,128]{1,0:T(8,128)} %c_hbm.1, f32[128,128]{1,0:T(8,128)} %s_hbm.1), custom_call_target="tpu_custom_call" | custom-call | tf_op jit(solution)/shard_map/pallas_call | solution.py:365
  59.8 2.0 %shard_map.77 = (f32[128,768]{1,0:T(8,128)}, f32[128,768]{1,0:T(8,128)}, f32[768]{0:T(1024)}) custom-call(f32[128,768]{1,0:T(8,128)} %get-tuple-element.6.first, f32[128,768]{1,0:T(8,128)} %get-tuple-element.7.second, f32[8,128]{1,0:T(8,128)} %get-tuple-element.8.explained), custom_call_target="tpu_custom_call" | custom-call | tf_op jit(solution)/shard_map/pallas_call | solution.py:405
